TPU v7x, 32 devices: a whole 2x2x4 slice. The times are simulated.
32 devices in a mesh: fsdp: 16 (over z, x, core), col: 2 (over y).
Axes of the slice: x: 2, y: 2, z: 4, core: 2. Of those that a mesh axis runs over, the one named last changes fastest.
Arguments:
- codes: bfloat16 [8192, 26624], P('fsdp', 'col'), may hold values from -96 to 96
- scales: float32 [64, 208], P('fsdp', 'col'), may hold values from 0.01 to 0.1
- factors: float32 [7, 8192, 64], P(None, 'fsdp'), may hold values from -0.225 to 0.225
- upstream: bfloat16 [8192, 26624], P('fsdp', 'col'), may hold values from -0.036621094 to 0.036621094
Outputs:
- factor_grads: float32 [7, 8192, 64], P(None, 'fsdp')
All inputs are finite; a program needn't handle non-finite values.
Results may differ from a plain program's by a relative error of at most 0.02.
Values may be sent and summed in bfloat16 or wider, within the bound.
A program may use at most 320 MiB of HBM per device.

v0:
```python
import jax
import jax.numpy as jnp
from jax import lax
from jax.sharding import PartitionSpec as P


def partner(block, axis, bit):
    count = lax.axis_size(axis)
    route = []
    for low in range(count):
        high = low | 1 << bit
        if high != low and high < count:
            route += [(low, high), (high, low)]
    return lax.ppermute(block, axis, route)


def rows_eye(first, count, distance, block):
    half = block // 2
    rows = first + jnp.arange(count, dtype=jnp.int32)
    pick = rows // distance % 2 * half + rows % half
    return (jnp.arange(block, dtype=jnp.int32)[None, :] == pick[:, None]).astype(jnp.float32)


def source_rows(first, count, distance, block):
    half = block // 2
    rows = first + jnp.arange(count, dtype=jnp.int32)
    inputs = jnp.arange(block, dtype=jnp.int32)
    group = rows // (2 * distance)
    part = rows % distance // half
    return (
        2 * distance * group[:, None]
        + distance * (inputs // half)[None, :]
        + half * part[:, None]
        + (inputs % half)[None, :]
    )


def dense_mixing(mixing, columns, width):
    onehot = columns[:, :, None] == jnp.arange(width, dtype=jnp.int32)[None, None, :]
    spread = jnp.where(onehot, mixing[:, :, None], jnp.zeros((), jnp.bfloat16))
    return jnp.sum(spread.astype(jnp.float32), axis=1).astype(jnp.bfloat16)


def left_product(matrix, grad):
    return lax.dot_general(
        matrix, grad, (((0,), (0,)), ((), ())), preferred_element_type=jnp.float32
    )


def local_scores(grad, values, distance, half):
    rows, wide = grad.shape
    groups = rows // (2 * distance)
    parts = distance // half
    grads = grad.reshape(groups, 2, parts, half, wide)
    vecs = values.reshape(groups, 2, parts, half, wide)
    out = jnp.einsum("ghqtc,gHqsc->ghqtHs", grads, vecs, preferred_element_type=jnp.float32)
    return out.reshape(rows, 2 * half)


def half_scores(grad, values, half):
    rows, wide = grad.shape
    grads = grad.reshape(rows // half, half, wide)
    vecs = values.reshape(rows // half, half, wide)
    out = jnp.einsum("qtc,qsc->qts", grads, vecs, preferred_element_type=jnp.float32)
    return out.reshape(rows, half)


def per_device(codes, scales, factors, upstream):
    rows, wide = codes.shape
    levels = factors.shape[0]
    block = factors.shape[2]
    half = block // 2
    scale_side = rows // scales.shape[0]
    index = lax.axis_index("fsdp")
    first = index * rows
    base = codes.astype(jnp.float32).reshape(
        rows // scale_side, scale_side, wide // scale_side, scale_side
    )
    base = (base * scales[:, None, :, None]).reshape(rows, wide).astype(jnp.bfloat16)
    row_ids = first + jnp.arange(rows, dtype=jnp.int32)
    plans = []
    for level in range(levels):
        distance = half * 2**level
        mixing = (rows_eye(first, rows, distance, block) + factors[level]).astype(jnp.bfloat16)
        sources = source_rows(first, rows, distance, block)
        if distance < rows:
            columns = sources - first
            matrix = dense_mixing(mixing, columns, rows)
            plans.append((matrix, None, None, None))
        else:
            stride = distance // rows
            bit = stride.bit_length() - 1
            side = index // stride % 2
            partner_first = first + distance * (1 - 2 * side)
            inside = (sources >= first) & (sources < first + rows)
            columns = jnp.where(inside, sources - first, sources - partner_first + rows)
            matrix = dense_mixing(mixing, columns, 2 * rows)
            plans.append((matrix[:, :rows], matrix[:, rows:], bit, side))
    values = base
    saved = []
    partners = []
    for level in range(levels):
        distance = half * 2**level
        matrix, far_matrix, bit, side = plans[level]
        saved.append(values)
        if distance < rows:
            partners.append(None)
            values = jnp.dot(matrix, values, preferred_element_type=jnp.float32).astype(
                jnp.bfloat16
            )
        else:
            other = partner(values, "fsdp", bit)
            partners.append(other)
            total = jnp.dot(matrix, values, preferred_element_type=jnp.float32)
            total = total + jnp.dot(far_matrix, other, preferred_element_type=jnp.float32)
            values = total.astype(jnp.bfloat16)
    grad = upstream
    results = [None] * levels
    for level in reversed(range(levels)):
        distance = half * 2**level
        matrix, far_matrix, bit, side = plans[level]
        if distance < rows:
            dmix = local_scores(grad, saved[level], distance, half)
            if level > 0:
                upper_rows = (row_ids // distance % 2 == 1)[:, None]
                low_matrix = jnp.where(upper_rows, jnp.zeros((), jnp.bfloat16), matrix)
                high_matrix = jnp.where(upper_rows, matrix, jnp.zeros((), jnp.bfloat16))
                lower = left_product(low_matrix, grad).astype(jnp.bfloat16)
                upper = left_product(high_matrix, grad).astype(jnp.bfloat16)
                grad = (lower.astype(jnp.float32) + upper.astype(jnp.float32)).astype(jnp.bfloat16)
        else:
            own_part = half_scores(grad, saved[level], half)
            far_part = half_scores(grad, partners[level], half)
            first_half = jnp.where(side == 0, own_part, far_part)
            second_half = jnp.where(side == 0, far_part, own_part)
            dmix = jnp.concatenate([first_half, second_half], axis=1)
            near_term = left_product(matrix, grad).astype(jnp.bfloat16)
            got_grad, got_matrix = partner((grad, far_matrix), "fsdp", bit)
            far_term = left_product(got_matrix, got_grad).astype(jnp.bfloat16)
            grad = (near_term.astype(jnp.float32) + far_term.astype(jnp.float32)).astype(
                jnp.bfloat16
            )
        results[level] = dmix
    stacked = jnp.stack(results)
    stacked = lax.psum(stacked, "col")
    return stacked


def solution(mesh):
    return jax.shard_map(
        per_device,
        mesh=mesh,
        in_specs=(P("fsdp", "col"), P("fsdp", "col"), P(None, "fsdp", None), P("fsdp", "col")),
        out_specs=P(None, "fsdp", None),
        check_vma=False,
    )
```

profile of v0, /device:TPU:0, one launch (start us, length us, event | category | flops | bytes accessed | tf_op | source)
XLA Modules:
  0.0 1352.8 jit_solution(15146822828176986559)
XLA Ops:
  7.0 2.0 fusion.67
  9.2 27.1 %fusion.3 = bf16[512,1024]{1,0:T(8,128)(2,1)S(1)} fusion(s32[512,64]{1,0:T(8,128)S(1)} %copy.78, bf16[512,64]{1,0:T(8,128)(2,1)S(1)} %copy.79), kind=kLoop, calls=%fused_computation.6 | loop fusion | flops 100139008 | bytes 1245184 | tf_op jit(solution)/shard_map/reduce_sum | solution.py:41
  36.3 0.8 slice.55
  37.1 3.0 collective-permute-start
  41.4 1.0 copy.82
  42.4 11.5 mul.287
  53.9 21.8 %fusion.14 = bf16[512,13312]{1,0:T(8,128)(2,1)} fusion(f32[64,8,104,128]{3,2,1,0:T(8,128)} %bitcast.166, bf16[512,13312]{1,0:T(8,128)(2,1)} %param.4), kind=kLoop, calls=%fused_computation.22 | loop fusion | flops 20447232 | bytes 54525952 | tf_op jit(solution)/shard_map/convert_element_type | solution.py:79
  75.7 15.2 %fusion.12 = bf16[512,512]{1,0:T(8,128)(2,1)S(1)} fusion(s32[512,64]{1,0:T(8,128)S(1)} %copy.70, bf16[512,64]{1,0:T(8,128)(2,1)S(1)} %copy.71), kind=kLoop, calls=%fused_computation.19 | loop fusion | flops 50069504 | bytes 720896 | tf_op jit(solution)/shard_map/reduce_sum | solution.py:41
  90.9 15.2 %fusion.13 = bf16[512,512]{1,0:T(8,128)(2,1)S(1)} fusion(s32[512,64]{1,0:T(8,128)S(1)} %copy.68, bf16[512,64]{1,0:T(8,128)(2,1)S(1)} %copy.69), kind=kLoop, calls=%fused_computation.20 | loop fusion | flops 50069504 | bytes 720896 | tf_op jit(solution)/shard_map/reduce_sum | solution.py:41
  106.0 15.2 %fusion.10 = bf16[512,512]{1,0:T(8,128)(2,1)S(1)} fusion(s32[512,64]{1,0:T(8,128)S(1)} %copy.81, bf16[512,64]{1,0:T(8,128)(2,1)S(1)} %copy.82), kind=kLoop, calls=%fused_computation.17 | loop fusion | flops 50069504 | bytes 720896 | tf_op jit(solution)/shard_map/reduce_sum | solution.py:41
  121.2 15.3 %convolution_convert_fusion.3 = bf16[512,13312]{1,0:T(8,128)(2,1)} fusion(bf16[512,512]{1,0:T(8,128)(2,1)S(1)} %fusion.10, bf16[512,13312]{1,0:T(8,128)(2,1)} %fusion.14), kind=kOutput, calls=%fused_computation.34 | convolution fusion | flops 6986137600 | bytes 27787264 | tf_op jit(solution)/shard_map/dot_general | solution.py:108
  136.5 15.2 %convolution_convert_fusion.2 = bf16[512,13312]{1,0:T(8,128)(2,1)} fusion(bf16[512,512]{1,0:T(8,128)(2,1)S(1)} %fusion.13, bf16[512,13312]{1,0:T(8,128)(2,1)} %convolution_convert_fusion.3), kind=kOutput, calls=%fused_computation.33 | convolution fusion | flops 6986137600 | bytes 27787264 | tf_op jit(solution)/shard_map/dot_general | solution.py:108
  151.7 15.2 %convolution_convert_fusion.1 = bf16[512,13312]{1,0:T(8,128)(2,1)} fusion(bf16[512,512]{1,0:T(8,128)(2,1)S(1)} %fusion.12, bf16[512,13312]{1,0:T(8,128)(2,1)} %convolution_convert_fusion.2), kind=kOutput, calls=%fused_computation.32 | convolution fusion | flops 6986137600 | bytes 27787264 | tf_op jit(solution)/shard_map/dot_general | solution.py:108
  166.9 15.2 %fusion.11 = bf16[512,512]{1,0:T(8,128)(2,1)S(1)} fusion(s32[512,64]{1,0:T(8,128)S(1)} %copy.72, bf16[512,64]{1,0:T(8,128)(2,1)S(1)} %copy.73), kind=kLoop, calls=%fused_computation.18 | loop fusion | flops 50069504 | bytes 720896 | tf_op jit(solution)/shard_map/reduce_sum | solution.py:41
  182.0 15.4 %convolution_convert_fusion = bf16[512,13312]{1,0:T(8,128)(2,1)} fusion(bf16[512,512]{1,0:T(8,128)(2,1)S(1)} %fusion.11, bf16[512,13312]{1,0:T(8,128)(2,1)} %convolution_convert_fusion.1), kind=kOutput, calls=%fused_computation.31 | convolution fusion | flops 6986137600 | bytes 27787264 | tf_op jit(solution)/shard_map/dot_general | solution.py:108
  197.7 27.1 %fusion.5 = bf16[512,1024]{1,0:T(8,128)(2,1)S(1)} fusion(s32[512,64]{1,0:T(8,128)S(1)} %copy.74, bf16[512,64]{1,0:T(8,128)(2,1)S(1)} %copy.75), kind=kLoop, calls=%fused_computation.8 | loop fusion | flops 100139008 | bytes 1245184 | tf_op jit(solution)/shard_map/reduce_sum | solution.py:41
  224.8 17.8 %fusion.55 = f32[512,13312]{1,0:T(8,128)} fusion(bf16[512,13312]{1,0:T(8,128)(2,1)} %convolution_convert_fusion, bf16[512,1024]{1,0:T(8,128)(2,1)S(1)} %fusion.5), kind=kOutput, calls=%fused_computation.76 | convolution fusion | flops 6979321856 | bytes 41418752 | tf_op jit(solution)/shard_map/dot_general | solution.py:114
  242.6 15.2 %convolution_convert_fusion.15 = bf16[512,13312]{1,0:T(8,128)(2,1)} fusion(bf16[512,13312]{1,0:T(8,128)(2,1)} %param.7, bf16[512,1024]{1,0:T(8,128)(2,1)S(1)} %fusion.3), kind=kOutput, calls=%fused_computation.46 | convolution fusion | flops 6986137600 | bytes 27787264 | tf_op jit(solution)/shard_map/dot_general | solution.py:45
  258.1 86.4 %collective-permute-done.1 = bf16[512,13312]{1,0:T(8,128)(2,1)} collective-permute-done((bf16[512,13312]{1,0:T(8,128)(2,1)}, bf16[512,13312]{1,0:T(8,128)(2,1)}, u32[]{:S(2)}, u32[]{:S(2)}) %collective-permute-start.1) | collective-permute-done | bytes 13631520 | tf_op jit(solution)/shard_map/ppermute | solution.py:14
  344.5 17.5 %add_convert_fusion.7 = bf16[512,13312]{1,0:T(8,128)(2,1)} fusion(bf16[512,13312]{1,0:T(8,128)(2,1)} %convolution_convert_fusion.15, bf16[512,512]{1,0:T(8,128)(2,1)S(1)} %collective-permute-done, bf16[512,13312]{1,0:T(8,128)(2,1)} %collective-permute-done.1), kind=kOutput, calls=%fused_computation.30 | convolution fusion | flops 7013400576 | bytes 41418752 | tf_op jit(solution)/shard_map/dot_general | solution.py:45
  362.0 1.7 collective-permute-start.3
  363.7 20.2 %add_convert_fusion.1 = bf16[512,13312]{1,0:T(8,128)(2,1)} fusion(f32[512,13312]{1,0:T(8,128)} %fusion.55, bf16[512,13312]{1,0:T(8,128)(2,1)} %collective-permute-done.6, bf16[512,1024]{1,0:T(8,128)(2,1)S(1)} %fusion.5), kind=kOutput, calls=%fused_computation.24 | convolution fusion | flops 6992953344 | bytes 55050240 | tf_op jit(solution)/shard_map/dot_general | solution.py:115
  384.3 27.1 %fusion.4 = bf16[512,1024]{1,0:T(8,128)(2,1)S(1)} fusion(s32[512,64]{1,0:T(8,128)S(1)} %copy.76, bf16[512,64]{1,0:T(8,128)(2,1)S(1)} %copy.77), kind=kLoop, calls=%fused_computation.7 | loop fusion | flops 100139008 | bytes 1245184 | tf_op jit(solution)/shard_map/reduce_sum | solution.py:41
  411.4 0.8 slice.56
  412.2 1.7 collective-permute-start.2
  413.9 0.8 slice.57
  414.7 0.6 broadcast_compare_fusion.2
  415.3 0.5 broadcast_compare_fusion
  415.8 15.2 %convolution_convert_fusion.13 = bf16[512,13312]{1,0:T(8,128)(2,1)} fusion(bf16[512,13312]{1,0:T(8,128)(2,1)} %add_convert_fusion.7, bf16[512,1024]{1,0:T(8,128)(2,1)S(1)} %fusion.4), kind=kOutput, calls=%fused_computation.44 | convolution fusion | flops 6986137600 | bytes 27787264 | tf_op jit(solution)/shard_map/dot_general | solution.py:45
  431.0 17.6 %fusion.52 = f32[512,13312]{1,0:T(8,128)} fusion(bf16[512,13312]{1,0:T(8,128)(2,1)} %add_convert_fusion.1, bf16[512,1024]{1,0:T(8,128)(2,1)S(1)} %fusion.4), kind=kOutput, calls=%fused_computation.73 | convolution fusion | flops 6979321856 | bytes 41418752 | tf_op jit(solution)/shard_map/dot_general | solution.py:114
  448.6 10.6 fusion.139
  459.2 500.3 %collective-permute-done.2 = bf16[512,512]{1,0:T(8,128)(2,1)S(1)} collective-permute-done((bf16[512,512]{1,0:T(8,128)(2,1)}, bf16[512,512]{1,0:T(8,128)(2,1)S(1)}, u32[]{:S(2)}, u32[]{:S(2)}) %collective-permute-start.2) | collective-permute-done | bytes 524320 | tf_op jit(solution)/shard_map/ppermute | solution.py:14
  959.6 17.5 %add_convert_fusion.6 = bf16[512,13312]{1,0:T(8,128)(2,1)} fusion(bf16[512,13312]{1,0:T(8,128)(2,1)} %convolution_convert_fusion.13, bf16[512,512]{1,0:T(8,128)(2,1)S(1)} %collective-permute-done.2, bf16[512,13312]{1,0:T(8,128)(2,1)} %collective-permute-done.3), kind=kOutput, calls=%fused_computation.29 | convolution fusion | flops 7013400576 | bytes 41418752 | tf_op jit(solution)/shard_map/dot_general | solution.py:45
  977.1 19.9 %add_convert_fusion = bf16[512,13312]{1,0:T(8,128)(2,1)} fusion(f32[512,13312]{1,0:T(8,128)} %fusion.52, bf16[512,13312]{1,0:T(8,128)(2,1)} %collective-permute-done.7, bf16[512,1024]{1,0:T(8,128)(2,1)S(1)} %fusion.4), kind=kOutput, calls=%fused_computation.23 | convolution fusion | flops 6992953344 | bytes 55050240 | tf_op jit(solution)/shard_map/dot_general | solution.py:115
  996.9 1.4 collective-permute-start.8
  998.4 10.7 fusion.138
  1009.1 10.7 broadcast_select_fusion.3
  1019.8 10.7 broadcast_select_fusion.1
  1030.4 15.5 %convolution_convert_fusion.11 = bf16[512,13312]{1,0:T(8,128)(2,1)} fusion(bf16[512,13312]{1,0:T(8,128)(2,1)} %add_convert_fusion.6, bf16[512,1024]{1,0:T(8,128)(2,1)S(1)} %fusion.5), kind=kOutput, calls=%fused_computation.42 | convolution fusion | flops 6986137600 | bytes 27787264 | tf_op jit(solution)/shard_map/dot_general | solution.py:45
  1045.9 11.4 fusion.140
  1057.3 0.7 copy.93
  1058.0 0.7 copy.92
  1058.7 0.7 copy.95
  1059.4 0.7 copy.94
  1060.2 17.5 %add_convert_fusion.5 = bf16[512,13312]{1,0:T(8,128)(2,1)} fusion(bf16[512,13312]{1,0:T(8,128)(2,1)} %convolution_convert_fusion.11, bf16[512,512]{1,0:T(8,128)(2,1)S(1)} %collective-permute-done.4, bf16[512,13312]{1,0:T(8,128)(2,1)} %collective-permute-done.5), kind=kOutput, calls=%fused_computation.28 | convolution fusion | flops 7013400576 | bytes 41418752 | tf_op jit(solution)/shard_map/dot_general | solution.py:45
  1077.6 15.8 %convolution_convert_fusion.8 = bf16[512,13312]{1,0:T(8,128)(2,1)} fusion(bf16[512,13312]{1,0:T(8,128)(2,1)} %add_convert_fusion.5, bf16[512,512]{1,0:T(8,128)(2,1)S(1)} %copy-done.5, pred[512]{0:T(512)(128)(4,1)S(1)} %copy-done.13), kind=kOutput, calls=%fused_computation.39 | convolution fusion | flops 6986399744 | bytes 27787776 | tf_op jit(solution)/shard_map/dot_general | solution.py:45
  1093.5 17.8 %add_convert_fusion.4 = bf16[512,13312]{1,0:T(8,128)(2,1)} fusion(bf16[512,13312]{1,0:T(8,128)(2,1)} %convolution_convert_fusion.8, bf16[512,13312]{1,0:T(8,128)(2,1)} %add_convert_fusion.5, bf16[512,512]{1,0:T(8,128)(2,1)S(1)} %copy-done.5, pred[512]{0:T(512)(128)(4,1)S(1)} %copy-done.13), kind=kOutput, calls=%fused_computation.27 | convolution fusion | flops 7013662720 | bytes 41419264 | tf_op jit(solution)/shard_map/dot_general | solution.py:45
  1111.2 15.3 %convolution_convert_fusion.6 = bf16[512,13312]{1,0:T(8,128)(2,1)} fusion(bf16[512,13312]{1,0:T(8,128)(2,1)} %add_convert_fusion.4, bf16[512,512]{1,0:T(8,128)(2,1)S(1)} %copy-done.3, pred[512]{0:T(512)(128)(4,1)S(1)} %copy-done.12), kind=kOutput, calls=%fused_computation.37 | convolution fusion | flops 6986399744 | bytes 27787776 | tf_op jit(solution)/shard_map/dot_general | solution.py:45
  1126.5 17.6 %add_convert_fusion.3 = bf16[512,13312]{1,0:T(8,128)(2,1)} fusion(bf16[512,13312]{1,0:T(8,128)(2,1)} %convolution_convert_fusion.6, bf16[512,13312]{1,0:T(8,128)(2,1)} %add_convert_fusion.4, bf16[512,512]{1,0:T(8,128)(2,1)S(1)} %copy-done.3, pred[512]{0:T(512)(128)(4,1)S(1)} %copy-done.12), kind=kOutput, calls=%fused_computation.26 | convolution fusion | flops 7013662720 | bytes 41419264 | tf_op jit(solution)/shard_map/dot_general | solution.py:45
  1144.2 15.3 %convolution_convert_fusion.4 = bf16[512,13312]{1,0:T(8,128)(2,1)} fusion(bf16[512,13312]{1,0:T(8,128)(2,1)} %add_convert_fusion.3, bf16[512,512]{1,0:T(8,128)(2,1)S(1)} %copy-done.1, pred[512]{0:T(512)(128)(4,1)S(1)} %copy-done.11), kind=kOutput, calls=%fused_computation.35 | convolution fusion | flops 6986399744 | bytes 27787776 | tf_op jit(solution)/shard_map/dot_general | solution.py:45
  1159.5 17.5 %add_convert_fusion.2 = bf16[512,13312]{1,0:T(8,128)(2,1)} fusion(bf16[512,13312]{1,0:T(8,128)(2,1)} %convolution_convert_fusion.4, bf16[512,13312]{1,0:T(8,128)(2,1)} %add_convert_fusion.3, bf16[512,512]{1,0:T(8,128)(2,1)S(1)} %copy-done.1, pred[512]{0:T(512)(128)(4,1)S(1)} %copy-done.11), kind=kOutput, calls=%fused_computation.25 | convolution fusion | flops 7013662720 | bytes 41419264 | tf_op jit(solution)/shard_map/dot_general | solution.py:45
  1177.0 28.8 %convolution_bitcast_fusion = f32[8,2,1,32,2,32]{3,5,1,4,0,2:T(8,128)S(1)} fusion(bf16[8,2,32,13312,1]{3,2,4,1,0:T(8,128)(2,1)} %bitcast.172, bf16[8,2,32,13312,1]{3,2,1,4,0:T(8,128)(2,1)} %bitcast.167), kind=kOutput, calls=%fused_computation.56 | convolution fusion | flops 872415232 | bytes 27394048 | tf_op jit(solution)/shard_map/ghqtc,gHqsc->ghqtHs/dot_general | solution.py:56
  1205.8 0.4 copy.80
  1206.2 0.7 stack_reshape.12
  1206.9 16.4 %fusion.24 = f32[4,2,2,32,2,32]{3,5,1,4,2,0:T(8,128)S(1)} fusion(bf16[4,2,2,32,13312,1]{4,3,2,1,0,5:T(8,128)(2,1)} %bitcast.160, bf16[4,2,2,32,13312,1]{4,3,2,1,0,5:T(8,128)(2,1)} %bitcast.179), kind=kOutput, calls=%fused_computation.57 | convolution fusion | flops 872415232 | bytes 27394048 | tf_op jit(solution)/shard_map/ghqtc,gHqsc->ghqtHs/dot_general | solution.py:56
  1223.7 0.7 stack_reshape.13
  1224.4 16.8 %fusion.29 = f32[2,2,4,32,2,32]{3,5,1,4,2,0:T(8,128)S(1)} fusion(bf16[2,2,4,32,13312,1]{4,3,2,1,0,5:T(8,128)(2,1)} %bitcast.159, bf16[2,2,4,32,13312,1]{4,3,2,1,0,5:T(8,128)(2,1)} %bitcast.178), kind=kOutput, calls=%fused_computation.58 | convolution fusion | flops 872415232 | bytes 27394048 | tf_op jit(solution)/shard_map/ghqtc,gHqsc->ghqtHs/dot_general | solution.py:56
  1241.5 0.4 stack_reshape.14
  1241.9 16.4 %fusion.34 = f32[1,2,8,32,2,32]{3,5,1,4,2,0:T(8,128)S(1)} fusion(bf16[2,8,32,13312,1]{3,2,1,0,4:T(8,128)(2,1)} %bitcast.158, bf16[2,8,32,13312,1]{3,2,1,0,4:T(8,128)(2,1)} %bitcast.177), kind=kOutput, calls=%fused_computation.59 | convolution fusion | flops 872415232 | bytes 27394048 | tf_op jit(solution)/shard_map/ghqtc,gHqsc->ghqtHs/dot_general | solution.py:56
  1258.9 33.5 %collective-permute-done.8 = bf16[512,13312]{1,0:T(8,128)(2,1)} collective-permute-done((bf16[512,13312]{1,0:T(8,128)(2,1)}, bf16[512,13312]{1,0:T(8,128)(2,1)}, u32[]{:S(2)}, u32[]{:S(2)}) %collective-permute-start.8) | collective-permute-done | bytes 13631520 | tf_op jit(solution)/shard_map/ppermute | solution.py:14
  1292.5 10.7 select_bitcast_fusion.1
  1304.0 0.9 copy-done.6
  1304.9 38.5 %all-reduce.2.cloned.1.call-done = f32[7,512,64]{1,2,0:T(8,128)} async-done(((f32[7,512,64]{1,2,0:T(8,128)}), f32[7,512,64]{1,2,0:T(8,128)}) %all-reduce.2.cloned.1.call-update) | async-done | bytes 917520 | tf_op jit(solution)/shard_map/psum | solution.py:145
  1343.3 2.2 copy.151
  (88 shorter events, 4.6 us)
Async XLA Ops:
  6.5 1336.8 %all-reduce.2.cloned.1.call-start = ((), (), s32[]{:S(2)}) async-start(), calls=%async_computation | async-start | bytes 1835008 | tf_op jit(solution)/shard_map/psum | solution.py:145
  37.1 221.0 %collective-permute-start = (bf16[512,512]{1,0:T(8,128)(2,1)}, bf16[512,512]{1,0:T(8,128)(2,1)S(1)}, u32[]{:S(2)}, u32[]{:S(2)}) collective-permute-start(bf16[512,512]{1,0:T(8,128)(2,1)} %slice.55), channel_id=1, source_target_pairs={{0,8},{8,0},{2,10},{10,2},{4,12},{12,4},{6,14},{14,6},{16,24},{24,... | collective-permute-start | bytes 1572872 | tf_op jit(solution)/shard_map/ppermute | solution.py:14
  40.1 304.4 %collective-permute-start.1 = (bf16[512,13312]{1,0:T(8,128)(2,1)}, bf16[512,13312]{1,0:T(8,128)(2,1)}, u32[]{:S(2)}, u32[]{:S(2)}) collective-permute-start(bf16[512,13312]{1,0:T(8,128)(2,1)} %param.7), channel_id=1, source_target_pairs={{0,8},{8,0},{2,10},{10,2},{4,12},{12,4},{6,14},{14,6},{16,24},{24,... | collective-permute-start | bytes 40894472 | tf_op jit(solution)/shard_map/ppermute | solution.py:14
  90.9 60.8 %copy-start.2 = (bf16[512,512]{1,0:T(8,128)(2,1)}, bf16[512,512]{1,0:T(8,128)(2,1)S(1)}, u32[]{:S(2)}) copy-start(bf16[512,512]{1,0:T(8,128)(2,1)S(1)} %fusion.12) | copy-start | bytes 1572868
  106.0 30.4 %copy-start = (bf16[512,512]{1,0:T(8,128)(2,1)}, bf16[512,512]{1,0:T(8,128)(2,1)S(1)}, u32[]{:S(2)}) copy-start(bf16[512,512]{1,0:T(8,128)(2,1)S(1)} %fusion.13) | copy-start | bytes 1572868
  182.0 15.4 %copy-start.4 = (bf16[512,512]{1,0:T(8,128)(2,1)}, bf16[512,512]{1,0:T(8,128)(2,1)S(1)}, u32[]{:S(2)}) copy-start(bf16[512,512]{1,0:T(8,128)(2,1)S(1)} %fusion.11) | copy-start | bytes 1572868
  197.4 166.3 %collective-permute-start.6 = (bf16[512,13312]{1,0:T(8,128)(2,1)}, bf16[512,13312]{1,0:T(8,128)(2,1)}, u32[]{:S(2)}, u32[]{:S(2)}) collective-permute-start(bf16[512,13312]{1,0:T(8,128)(2,1)} %convolution_convert_fusion), channel_id=1, source_target_pairs={{0,2},{2,0},{4,6},{6,4},{8,10},{10,8},{12,14},{14,12},{16,18},{18,... | collective-permute-start | bytes 40894472 | tf_op jit(solution)/shard_map/ppermute | solution.py:14
  362.0 597.6 %collective-permute-start.3 = (bf16[512,13312]{1,0:T(8,128)(2,1)}, bf16[512,13312]{1,0:T(8,128)(2,1)}, u32[]{:S(2)}, u32[]{:S(2)}) collective-permute-start(bf16[512,13312]{1,0:T(8,128)(2,1)} %add_convert_fusion.7), channel_id=1, source_target_pairs={{0,4},{4,0},{2,6},{6,2},{8,12},{12,8},{10,14},{14,10},{16,20},{20,... | collective-permute-start | bytes 40894472 | tf_op jit(solution)/shard_map/ppermute | solution.py:14
  383.9 593.1 %collective-permute-start.7 = (bf16[512,13312]{1,0:T(8,128)(2,1)}, bf16[512,13312]{1,0:T(8,128)(2,1)}, u32[]{:S(2)}, u32[]{:S(2)}) collective-permute-start(bf16[512,13312]{1,0:T(8,128)(2,1)} %add_convert_fusion.1), channel_id=1, source_target_pairs={{0,4},{4,0},{2,6},{6,2},{8,12},{12,8},{10,14},{14,10},{16,20},{20,... | collective-permute-start | bytes 40894472 | tf_op jit(solution)/shard_map/ppermute | solution.py:14
  412.2 547.4 %collective-permute-start.2 = (bf16[512,512]{1,0:T(8,128)(2,1)}, bf16[512,512]{1,0:T(8,128)(2,1)S(1)}, u32[]{:S(2)}, u32[]{:S(2)}) collective-permute-start(bf16[512,512]{1,0:T(8,128)(2,1)} %slice.56), channel_id=1, source_target_pairs={{0,4},{4,0},{2,6},{6,2},{8,12},{12,8},{10,14},{14,10},{16,20},{20,... | collective-permute-start | bytes 1572872 | tf_op jit(solution)/shard_map/ppermute | solution.py:14
  414.7 645.5 %collective-permute-start.4 = (bf16[512,512]{1,0:T(8,128)(2,1)}, bf16[512,512]{1,0:T(8,128)(2,1)S(1)}, u32[]{:S(2)}, u32[]{:S(2)}) collective-permute-start(bf16[512,512]{1,0:T(8,128)(2,1)} %slice.57), channel_id=1, source_target_pairs={{0,2},{2,0},{4,6},{6,4},{8,10},{10,8},{12,14},{14,12},{16,18},{18,... | collective-permute-start | bytes 1572872 | tf_op jit(solution)/shard_map/ppermute | solution.py:14
  977.1 83.1 %collective-permute-start.5 = (bf16[512,13312]{1,0:T(8,128)(2,1)}, bf16[512,13312]{1,0:T(8,128)(2,1)}, u32[]{:S(2)}, u32[]{:S(2)}) collective-permute-start(bf16[512,13312]{1,0:T(8,128)(2,1)} %add_convert_fusion.6), channel_id=1, source_target_pairs={{0,2},{2,0},{4,6},{6,4},{8,10},{10,8},{12,14},{14,12},{16,18},{18,... | collective-permute-start | bytes 40894472 | tf_op jit(solution)/shard_map/ppermute | solution.py:14
  996.9 295.5 %collective-permute-start.8 = (bf16[512,13312]{1,0:T(8,128)(2,1)}, bf16[512,13312]{1,0:T(8,128)(2,1)}, u32[]{:S(2)}, u32[]{:S(2)}) collective-permute-start(bf16[512,13312]{1,0:T(8,128)(2,1)} %add_convert_fusion), channel_id=1, source_target_pairs={{0,8},{8,0},{2,10},{10,2},{4,12},{12,4},{6,14},{14,6},{16,24},{24,... | collective-permute-start | bytes 40894472 | tf_op jit(solution)/shard_map/ppermute | solution.py:14
  1060.2 17.5 %copy-start.5 = (bf16[512,512]{1,0:T(8,128)(2,1)S(1)}, bf16[512,512]{1,0:T(8,128)(2,1)}, u32[]{:S(2)}) copy-start(bf16[512,512]{1,0:T(8,128)(2,1)} %copy-done.4) | copy-start | bytes 1572868
  1060.2 17.5 %copy-start.13 = (pred[512]{0:T(512)(128)(4,1)S(1)}, pred[512]{0:T(512)(128)(4,1)}, u32[]{:S(2)}) copy-start(pred[512]{0:T(512)(128)(4,1)} %get-tuple-element.45) | copy-start | bytes 1540
  1093.5 17.8 %copy-start.3 = (bf16[512,512]{1,0:T(8,128)(2,1)S(1)}, bf16[512,512]{1,0:T(8,128)(2,1)}, u32[]{:S(2)}) copy-start(bf16[512,512]{1,0:T(8,128)(2,1)} %copy-done.2) | copy-start | bytes 1572868
  1093.5 17.8 %copy-start.12 = (pred[512]{0:T(512)(128)(4,1)S(1)}, pred[512]{0:T(512)(128)(4,1)}, u32[]{:S(2)}) copy-start(pred[512]{0:T(512)(128)(4,1)} %get-tuple-element.46) | copy-start | bytes 1540
  1126.5 17.7 %copy-start.1 = (bf16[512,512]{1,0:T(8,128)(2,1)S(1)}, bf16[512,512]{1,0:T(8,128)(2,1)}, u32[]{:S(2)}) copy-start(bf16[512,512]{1,0:T(8,128)(2,1)} %copy-done) | copy-start | bytes 1572868
  1126.5 17.7 %copy-start.11 = (pred[512]{0:T(512)(128)(4,1)S(1)}, pred[512]{0:T(512)(128)(4,1)}, u32[]{:S(2)}) copy-start(pred[512]{0:T(512)(128)(4,1)} %broadcast_compare_fusion.2) | copy-start | bytes 1540
  1241.9 50.5 %copy-start.14 = (f32[16,32,32]{2,1,0:T(8,128)S(1)}, f32[16,32,32]{2,1,0:T(8,128)}, u32[]{:S(2)}) copy-start(f32[16,32,32]{2,1,0:T(8,128)} %fusion.140) | copy-start | bytes 196612
  1292.5 11.4 copy-start.7
  1292.5 11.4 copy-start.9
  1292.5 11.4 copy-start.8
  1292.5 11.4 copy-start.10
  1303.9 0.9 copy-start.6
Sparse Core Ops, SparseCore 0:
  1305.0 38.2 all-reduce.1
where the time goes:
time: 1360 us; the launch traced here: 1350 us
  waiting for transfers between devices  659 us (48%)
  matrix products  477 us (35%)
  other arithmetic  167 us (12%)
  local copies, waits for them, and re-layouts  26.7 us (2%)
  between operations  14.4 us (1%)
    ppermute x9, waiting for transfers between devices, partner(): return lax.ppermute(block, axis, route)  620 us
    dot_general x12, matrix products, left_product(): lax.dot_general(matrix, grad, (((0,), (0,)), ((), ())), preferred_element...  198 us
    reduce_sum x7, other arithmetic, dense_mixing(): return jnp.sum(spread.astype(jnp.float32), axis=1).astype(jnp.bfloat16)  142 us
    dot_general x4, matrix products, local_scores(): jnp.einsum('ghqtc,gHqsc->ghqtHs', grads, vecs, preferred_element_type=jnp...  78.4 us
    dot_general x6, matrix products, half_scores(): jnp.einsum('qtc,qsc->qts', grads, vecs, preferred_element_type=jnp.float32)  64.8 us
    dot_general x4, matrix products, per_device(): jnp.dot(matrix, values, preferred_element_type=jnp.float32)  61 us
    dot_general x2, matrix products, per_device(): jnp.dot(far_matrix, other, preferred_element_type=jnp.float32)  40.1 us
    psum x1, waiting for transfers between devices, per_device(): stacked = lax.psum(stacked, 'col')  38.5 us
  transfers between devices with their start and end apart: 10, of which 4 were waited for; matrix products, arithmetic and copies ran while one was open for 46% of the time, Pallas kernels for 0%

commit v1 on v0

--- a/solution.py
+++ b/solution.py
@@ -1,7 +1,14 @@
+import functools
+
 import jax
 import jax.numpy as jnp
 from jax import lax
+from jax.experimental import pallas as pl
+from jax.experimental.pallas import tpu as pltpu
 from jax.sharding import PartitionSpec as P
+
+MESH = pl.DeviceIdType.MESH
+LANES = 128
 
 
 def partner(block, axis, bit):
@@ -146,9 +153,323 @@
     return stacked
 
 
+def flipped(me, mask):
+    out, bit = me, 1
+    while bit <= mask:
+        if mask & bit:
+            out = out + bit * (1 - 2 * lax.rem(lax.div(me, bit), 2))
+        bit *= 2
+    return out
+
+
+def greet(partners):
+    barrier = pltpu.get_barrier_semaphore()
+    for device in partners:
+        pl.semaphore_signal(barrier, inc=1, device_id=device, device_id_type=MESH)
+    pl.semaphore_wait(barrier, len(partners))
+
+
+def exchange_kernel(
+    n, codes_ref, up_ref, mix_ref, scale_ref,
+    codes_out, up_out, mix_out, scale_out,
+    send_sem, recv_sem, own_sem,
+):
+    index = lax.axis_index("fsdp")
+    me = lax.rem(index, n)
+    wide = codes_out.shape[2]
+    device = lambda mask: {"fsdp": index - me + flipped(me, mask)}
+    greet([device(mask) for mask in range(1, n)])
+
+    def columns(place):
+        return pl.ds(pl.multiple_of(place * wide, LANES), wide)
+
+    def send(kind, mask, src, dst, to):
+        copy = pltpu.make_async_remote_copy(
+            src_ref=src,
+            dst_ref=dst,
+            send_sem=send_sem.at[kind, mask],
+            recv_sem=recv_sem.at[kind, mask],
+            device_id=device(to),
+            device_id_type=MESH,
+        )
+        copy.start()
+        return copy
+
+    local = [
+        pltpu.make_async_copy(mix_ref, mix_out.at[me], own_sem.at[0]),
+        pltpu.make_async_copy(scale_ref, scale_out.at[me], own_sem.at[1]),
+        pltpu.make_async_copy(codes_ref.at[:, columns(me)], codes_out.at[me], own_sem.at[2]),
+        pltpu.make_async_copy(up_ref.at[:, :, columns(me)], up_out.at[:, me], own_sem.at[3]),
+    ]
+    for copy in local:
+        copy.start()
+    copies, mixes = [], {}
+    for mask in list(range(2, n, 2)) + [1]:
+        mixes[mask] = send(0, mask, mix_ref, mix_out.at[me], mask)
+    order = sorted(range(1, n), key=lambda mask: -mask)
+    for mask in order:
+        copies.append(send(1, mask, scale_ref, scale_out.at[me], mask))
+    for mask in order:
+        src = up_ref.at[:, :, columns(flipped(me, mask))]
+        copies.append(send(2, mask, src, up_out.at[:, me], mask))
+    for mask in order:
+        src = codes_ref.at[:, columns(flipped(me, mask))]
+        copies.append(send(3, mask, src, codes_out.at[me], mask))
+    for mask in range(2, n, 2):
+        mixes[mask].wait()
+        block = mix_out.at[flipped(me, mask)]
+        copies.append(send(0, mask + 1, block, block, 1))
+    mixes[1].wait()
+    for copy in copies + local:
+        copy.wait()
+
+
+def exchange(n, codes, upstream, mixing, scales, half):
+    rows, cols = codes.shape
+    wide = cols // n
+    parts = rows // half
+    any_space = pl.BlockSpec(memory_space=pl.ANY)
+    shapes = (
+        jax.ShapeDtypeStruct((n, rows, wide), codes.dtype),
+        jax.ShapeDtypeStruct((parts, n, half, wide), upstream.dtype),
+        jax.ShapeDtypeStruct((n,) + mixing.shape, mixing.dtype),
+        jax.ShapeDtypeStruct((n,) + scales.shape, scales.dtype),
+    )
+    return pl.pallas_call(
+        functools.partial(exchange_kernel, n),
+        out_shape=shapes,
+        in_specs=[any_space] * 4,
+        out_specs=[any_space] * 4,
+        scratch_shapes=[
+            pltpu.SemaphoreType.DMA((4, n)),
+            pltpu.SemaphoreType.DMA((4, n)),
+            pltpu.SemaphoreType.DMA((4,)),
+        ],
+        compiler_params=pltpu.CompilerParams(collective_id=0, has_side_effects=True),
+        cost_estimate=pl.CostEstimate(
+            flops=0, bytes_accessed=8 * rows * cols, transcendentals=0
+        ),
+    )(codes, upstream.reshape(parts, half, cols), mixing, scales)
+
+
+def reduce_kernel(n, part_ref, out_ref, near, held, far, send_sem, recv_sem):
+    index = lax.axis_index("fsdp")
+    me = lax.rem(index, n)
+    device = lambda mask: {"fsdp": index - me + flipped(me, mask)}
+    masks = list(range(0, n, 2))
+    greet([device(mask) for mask in [1] + masks[1:]])
+    rows = out_ref.shape[0]
+    step = 64
+
+    def send(slot, src, dst, to):
+        copy = pltpu.make_async_remote_copy(
+            src_ref=src,
+            dst_ref=dst,
+            send_sem=send_sem.at[slot],
+            recv_sem=recv_sem.at[slot],
+            device_id=device(to),
+            device_id_type=MESH,
+        )
+        copy.start()
+        return copy
+
+    order = masks[::-1]
+    first = {
+        mask: send(mask, part_ref.at[flipped(me, mask + 1)], near.at[mask // 2], 1)
+        for mask in order
+    }
+    second = []
+    for mask in order:
+        first[mask].wait_recv()
+        own = flipped(me, mask)
+
+        def add(i, carry, mask=mask, own=own):
+            at = pl.ds(pl.multiple_of(i * step, step), step)
+            total = part_ref[own, at].astype(jnp.float32) + near[mask // 2, at].astype(
+                jnp.float32
+            )
+            if mask:
+                held[mask // 2 - 1, at] = total.astype(held.dtype)
+            else:
+                out_ref[at] = total
+            return carry
+
+        lax.fori_loop(0, rows // step, add, 0)
+        if mask:
+            second.append(
+                send(mask + 1, held.at[mask // 2 - 1], far.at[mask // 2 - 1], mask)
+            )
+    for copy in second:
+        copy.wait_recv()
+
+    def finish(i, carry):
+        at = pl.ds(pl.multiple_of(i * step, step), step)
+        total = out_ref[at]
+        for slot in range(n // 2 - 1):
+            total = total + far[slot, at].astype(jnp.float32)
+        out_ref[at] = total
+        return carry
+
+    lax.fori_loop(0, rows // step, finish, 0)
+    for copy in list(first.values()) + second:
+        copy.wait_send()
+
+
+def reduce_parts(n, parts):
+    _, rows, wide = parts.shape
+    return pl.pallas_call(
+        functools.partial(reduce_kernel, n),
+        out_shape=jax.ShapeDtypeStruct((rows, wide), jnp.float32),
+        in_specs=[pl.BlockSpec(memory_space=pltpu.VMEM)],
+        out_specs=pl.BlockSpec(memory_space=pltpu.VMEM),
+        scratch_shapes=[
+            pltpu.VMEM((n // 2, rows, wide), parts.dtype),
+            pltpu.VMEM((n // 2 - 1, rows, wide), parts.dtype),
+            pltpu.VMEM((n // 2 - 1, rows, wide), parts.dtype),
+            pltpu.SemaphoreType.DMA((n,)),
+            pltpu.SemaphoreType.DMA((n,)),
+        ],
+        compiler_params=pltpu.CompilerParams(
+            collective_id=1, has_side_effects=True, vmem_limit_bytes=40 * 2**20
+        ),
+    )(parts)
+
+
+def block_mask(count, half, bit, side, dtype):
+    rows = lax.broadcasted_iota(jnp.int32, (count, count), 0) // half
+    cols = lax.broadcasted_iota(jnp.int32, (count, count), 1) // half
+    low = rows // 2**bit % 2
+    return (cols == rows + (side - low) * 2**bit).astype(dtype)
+
+
+def repeat_eye(count, half, dtype):
+    place = lax.broadcasted_iota(jnp.int32, (half, count), 1) % half
+    return (place == lax.broadcasted_iota(jnp.int32, (half, count), 0)).astype(dtype)
+
+
+def spread(mix, bit):
+    count, half = mix.shape[-2], mix.shape[-1] // 2
+    eye = repeat_eye(count, half, jnp.bfloat16)
+    wide = [
+        jnp.einsum(
+            "...ts,sc->...tc", mix[..., side * half : (side + 1) * half], eye,
+            preferred_element_type=jnp.float32,
+        )
+        * block_mask(count, half, bit, side, jnp.float32)
+        for side in range(2)
+    ]
+    return (wide[0] + wide[1]).astype(jnp.bfloat16)
+
+
+def gather_back(full, bit, half):
+    count = full.shape[-1]
+    eye = repeat_eye(count, half, jnp.float32)
+    return jnp.concatenate(
+        [
+            jnp.einsum(
+                "...tc,sc->...ts", full * block_mask(count, half, bit, side, jnp.float32), eye,
+                preferred_element_type=jnp.float32, precision=lax.Precision.HIGHEST,
+            )
+            for side in range(2)
+        ],
+        axis=-1,
+    )
+
+
+def product(spec, left, right):
+    return jnp.einsum(
+        spec, left.astype(jnp.bfloat16), right.astype(jnp.bfloat16),
+        preferred_element_type=jnp.float32,
+    )
+
+
+def chain(mats):
+    prefix = [None, mats[0]]
+    for mat in mats[1:]:
+        prefix.append(product("...ij,...jk->...ik", mat, prefix[-1]).astype(jnp.bfloat16))
+    return prefix
+
+
+def level_grads(gram, mats, prefix, half):
+    out = [None] * len(mats)
+    left = gram
+    for bit in reversed(range(len(mats))):
+        full = left
+        if bit:
+            full = product("...ij,...kj->...ik", left, prefix[bit])
+            left = product("...ji,...jk->...ik", mats[bit], left)
+        out[bit] = gather_back(full, bit, half)
+    return out
+
+
+def per_device_columns(n, codes, scales, factors, upstream):
+    rows, cols = codes.shape
+    levels, _, block = factors.shape
+    half = block // 2
+    parts = rows // half
+    low = parts.bit_length() - 1
+    wide = cols // n
+    scale_rows, scale_cols = scales.shape
+    side = rows // scale_rows
+    index = lax.axis_index("fsdp")
+    me = index % n
+    first = index * rows
+    mixing = jnp.stack(
+        [
+            (rows_eye(first, rows, half * 2**level, block) + factors[level]).astype(jnp.bfloat16)
+            for level in range(levels)
+        ]
+    )
+    packed = mixing.reshape(levels * rows * block // LANES, LANES)
+    padded = jnp.pad(scales, ((0, -scale_rows % 8), (0, -scale_cols % LANES)))
+    codes_all, up, packed_all, scales_all = exchange(n, codes, upstream, packed, padded, half)
+    mix_all = packed_all.reshape(n, levels, rows, block)
+
+    scale = lax.dynamic_slice_in_dim(scales_all[:, :scale_rows], me * (wide // side), wide // side, 2)
+    base = codes_all.astype(jnp.float32).reshape(n, scale_rows, side, wide // side, side)
+    base = (base * scale[:, :, None, :, None]).astype(jnp.bfloat16).reshape(n, rows, wide)
+
+    inner = [spread(mix_all[:, level], level) for level in range(low)]
+    inner_prefix = chain(inner)
+    outer_mix = mix_all[:, low:].reshape(n, levels - low, parts, half, block)
+    outer_mix = outer_mix.transpose(1, 2, 0, 3, 4).reshape(levels - low, parts, n * half, block)
+    outer = [spread(outer_mix[bit], bit) for bit in range(levels - low)]
+    outer_prefix = chain(outer)
+
+    up = up.reshape(parts, n * half, wide)
+    grad = product("qji,qjc->qic", outer_prefix[-1], up).astype(jnp.bfloat16)
+    grad = grad.reshape(parts, n, half, wide).transpose(1, 0, 2, 3).reshape(n, rows, wide)
+    values = product("nij,njc->nic", inner_prefix[-1], base).astype(jnp.bfloat16)
+    values = values.reshape(n, parts, half, wide).transpose(1, 0, 2, 3)
+    values = values.reshape(parts, n * half, wide)
+    inner_gram = product("nic,njc->nij", grad, base)
+    outer_gram = product("qic,qjc->qij", up, values)
+    upper = jnp.concatenate(level_grads(outer_gram, outer, outer_prefix, half), axis=-1)
+    upper = upper.reshape(parts, n, half, -1).transpose(1, 0, 2, 3).reshape(n, rows, -1)
+
+    partial = jnp.concatenate([inner_gram, upper], axis=2).astype(jnp.bfloat16)
+    total = reduce_parts(n, partial)
+    own = [spread(mixing[level], level) for level in range(low)]
+    lower = level_grads(total[:, :rows], own, chain(own), half)
+    upper = total[:, rows:].reshape(rows, levels - low, block).transpose(1, 0, 2)
+    stacked = jnp.concatenate([jnp.stack(lower), upper], axis=0)
+    return lax.psum(stacked, "col")
+
+
+def body(codes, scales, factors, upstream):
+    rows, cols = codes.shape
+    levels, _, block = factors.shape
+    n = block * 2 ** (levels - 1) // rows
+    side = rows // scales.shape[0]
+    fits = n > 2 and rows % LANES == 0 and cols % (n * LANES) == 0 and cols % (n * side) == 0
+    if fits:
+        return per_device_columns(n, codes, scales, factors, upstream)
+    return per_device(codes, scales, factors, upstream)
+
+
 def solution(mesh):
     return jax.shard_map(
-        per_device,
+        body,
         mesh=mesh,
         in_specs=(P("fsdp", "col"), P("fsdp", "col"), P(None, "fsdp", None), P("fsdp", "col")),
         out_specs=P(None, "fsdp", None),

time: 1360 us -> 748 us (0.55)
  waiting for transfers between devices: 659 us -> 37.6 us
  Pallas kernels: 0 us -> 359 us
  matrix products: 477 us -> 191 us
  other arithmetic: 167 us -> 16.9 us
  local copies, waits for them, and re-layouts: 26.7 us -> 119 us
    ppermute x9 -> x0, waiting for transfers between devices: 620 us -> none  [partner(): return lax.ppermute(block, axis, route)]
    pallas_call x0 -> x2, Pallas kernels: none -> 359 us  [the longest x1 319 us: exchange(): pl.pallas_call(functools.partial(exchange_kernel, n), out_shape=shapes, i...]
    dot_general x30 -> x50, matrix products: 477 us -> 191 us  [the longest x19 125 us: product(): jnp.einsum(spec, left.astype(jnp.bfloat16), right.astype(jnp.bfloat16), p...]
    reduce_sum x7 -> x0, other arithmetic: 142 us -> none  [dense_mixing(): return jnp.sum(spread.astype(jnp.float32), axis=1).astype(jnp.bfloat16)]
    mul x1 -> x3, local copies, waits for them, and re-layouts: 11.5 us -> 67.2 us  [per_device_columns(): base * scale[:, :, None, :, None]]
    transpose x4 -> x3, local copies, waits for them, and re-layouts: 1.48 us -> 22.1 us  [the longest x1 10.3 us: per_device_columns(): grad.reshape(parts, n, half, wide).transpose(1, 0, 2, 3)]
    convert_element_type x2 -> x3, other arithmetic: 23.8 us -> 6.5 us  [the longest x2 4.66 us: block_mask(): return (cols == rows + (side - low) * 2 ** bit).astype(dtype)]
  transfers between devices with their start and end apart: 10 -> 1, of which waited for: 4 -> 1; matrix products, arithmetic and copies ran while one was open for 46% -> 0% of each run, Pallas kernels for 0% -> 0%
where the time goes in v1:
time: 748 us; the launch traced here: 737 us
  Pallas kernels  359 us (48%)
  matrix products  191 us (26%)
  local copies, waits for them, and re-layouts  119 us (16%)
  waiting for transfers between devices  37.6 us (5%)
  other arithmetic  16.9 us (2%)
  between operations  14.3 us (2%)
    pallas_call x1, Pallas kernels, exchange(): pl.pallas_call(functools.partial(exchange_kernel, n), out_shape=shapes, i...  319 us
    dot_general x19, matrix products, product(): jnp.einsum(spec, left.astype(jnp.bfloat16), right.astype(jnp.bfloat16), p...  125 us
    mul x3, local copies, waits for them, and re-layouts, per_device_columns(): base * scale[:, :, None, :, None]  67.2 us
    pallas_call x1, Pallas kernels, reduce_parts(): pl.pallas_call(functools.partial(reduce_kernel, n), out_shape=jax.ShapeDt...  40.1 us
    psum x1, waiting for transfers between devices, per_device_columns(): return lax.psum(stacked, 'col')  37.6 us
    dot_general x17, matrix products, spread(): jnp.einsum('...ts,sc->...tc', mix[..., side * half:(side + 1) * half], ey...  37.2 us
    dot_general x14, matrix products, gather_back(): jnp.einsum('...tc,sc->...ts', full * block_mask(count, half, bit, side, j...  28.9 us
  transfers between devices with their start and end apart: 1, of which 1 were waited for; matrix products, arithmetic and copies ran while one was open for 0% of the time, Pallas kernels for 0%

profile of v1, /device:TPU:0, one launch (start us, length us, event | category | flops | bytes accessed | tf_op | source)
XLA Modules:
  0.0 737.0 jit_solution(16135544221155305607)
XLA Ops:
  6.8 0.9 fusion.185
  7.7 0.9 fusion.186
  8.6 1.8 fusion.173
  10.5 0.9 fusion.187
  11.4 0.9 fusion.188
  12.3 0.9 fusion.189
  13.3 0.9 fusion.190
  14.2 0.9 fusion.191
  15.5 1.2 reshape.1724.mix_ref
  17.3 318.7 %shard_map.46 = (bf16[8,512,1664]{2,1,0:T(8,128)(2,1)}, bf16[16,8,32,1664]{3,2,1,0:T(8,128)(2,1)}, bf16[8,1792,128]{2,1,0:T(8,128)(2,1)}, f32[8,8,128]{2,1,0:T(8,128)}) custom-call(bf16[512,13312]{1,0:T(8,128)(2,1)} %codes_ref.1, bf16[16,32,13312]{2,1,0:T(8,128)(2,1)} %bitcast.130, bf16[1792,128]{1,0:T(8,128)(2,1)} %reshape.1724.mix_ref, f32[8,128]{1,0:T(8,128)} %pad.4.scale_ref), custom_call_target="tpu_custom_call" | custom-call | bytes 54525952 | tf_op jit(solution)/shard_map/pallas_call | solution.py:238
  336.1 10.1 %reshape.1725 = bf16[8,7,512,64]{3,2,1,0:T(8,128)(2,1)} reshape(bf16[8,1792,128]{2,1,0:T(8,128)(2,1)} %get-tuple-element.9) | data formatting | bytes 7340032 | tf_op jit(solution)/shard_map/reshape | solution.py:426
  346.1 4.4 slice_bitcast_fusion
  350.5 0.9 copy.42
  352.0 2.7 fusion.120
  354.7 2.7 fusion.123
  357.3 4.6 fusion.114
  361.9 4.6 fusion.110
  366.6 4.5 fusion.106
  371.0 4.6 fusion.102
  375.8 9.5 %mul.429 = f32[8,4,128,13,128]{2,1,4,3,0:T(4,128)} broadcast(f32[8,4,13]{1,2,0:T(8,128)S(1)} %copy.23), dimensions={0,1,3} | broadcast | bytes 27264640 | tf_op jit(solution)/shard_map/mul | solution.py:430
  385.3 31.9 %mul.430 = f32[8,512,1664]{1,2,0:T(8,128)} reshape(f32[8,4,128,13,128]{2,1,4,3,0:T(4,128)} %mul.429) | data formatting | bytes 54525952 | tf_op jit(solution)/shard_map/mul | solution.py:430
  417.2 25.8 %copy.24 = f32[8,512,1664]{2,1,0:T(8,128)} copy(f32[8,512,1664]{1,2,0:T(8,128)} %mul.430) | data formatting | bytes 54525952 | tf_op jit(solution)/shard_map/mul | solution.py:430
  443.0 4.2 fusion.182
  447.1 15.7 %fusion.2 = bf16[8,512,512]{2,1,0:T(8,128)(2,1)} fusion(f32[8,512,512]{2,1,0:T(8,128)} %fusion.106, f32[8,512,512]{2,1,0:T(8,128)} %fusion.102, f32[512,512]{1,0:T(8,128)} %get-tuple-element.31, f32[512,512]{1,0:T(8,128)} %get-tuple-element.30, f32[512,512]{1,0:T(8,128)} %get-tuple-element.28, f32[512,512]{1,0:T(8,128)} %get-tuple-element.29, ...), kind=kOutput, calls=%fused_computation.30 | convolution fusion | flops 2432761856 | bytes 26223616 | tf_op jit(solution)/shard_map/...ij,...jk->...ik/dot_general | solution.py:380
  462.9 9.2 %fusion.1 = bf16[8,512,512]{2,1,0:T(8,128)(2,1)} fusion(f32[8,512,512]{2,1,0:T(8,128)} %fusion.110, bf16[8,512,512]{2,1,0:T(8,128)(2,1)} %fusion.2, f32[512,512]{1,0:T(8,128)} %get-tuple-element.26, f32[512,512]{1,0:T(8,128)} %get-tuple-element.27, bf16[8,512,64]{2,1,0:T(8,128)(2,1)S(1)} %copy-done.10, s32[512]{0:T(512)S(1)} %get-tuple-element.45, ...), kind=kOutput, calls=%fused_computation.29 | convolution fusion | flops 2290122752 | bytes 19403264 | tf_op jit(solution)/shard_map/...ij,...jk->...ik/dot_general | solution.py:380
  472.1 9.1 %fusion = bf16[8,512,512]{2,1,0:T(8,128)(2,1)} fusion(f32[8,512,512]{2,1,0:T(8,128)} %fusion.114, bf16[8,512,512]{2,1,0:T(8,128)(2,1)} %fusion.1, f32[512,512]{1,0:T(8,128)} %get-tuple-element.25, f32[512,512]{1,0:T(8,128)} %get-tuple-element.24, bf16[8,512,64]{2,1,0:T(8,128)(2,1)S(1)} %copy-done.9, s32[512]{0:T(512)S(1)} %get-tuple-element.45, ...), kind=kOutput, calls=%fused_computation.28 | convolution fusion | flops 2290122752 | bytes 19403264 | tf_op jit(solution)/shard_map/...ij,...jk->...ik/dot_general | solution.py:380
  481.2 21.3 %convolution_convert_fusion = bf16[8,512,1664]{2,1,0:T(8,128)(2,1)} fusion(bf16[8,512,512]{2,1,0:T(8,128)(2,1)} %fusion, f32[8,512,1664]{2,1,0:T(8,128)} %copy.24, bf16[8,512,1664]{2,1,0:T(8,128)(2,1)} %get-tuple-element.11), kind=kOutput, calls=%fused_computation.1 | convolution fusion | flops 7006584832 | bytes 58720256 | tf_op jit(solution)/shard_map/nij,njc->nic/dot_general | solution.py:380
  502.5 10.2 %copy.26 = bf16[16,8,32,1664]{3,2,1,0:T(8,128)(2,1)} copy(bf16[16,8,32,1664]{3,2,0,1:T(8,128)(2,1)} %bitcast.126) | data formatting | bytes 27262976 | tf_op jit(solution)/shard_map/transpose | solution.py:443
  512.7 2.6 fusion.117
  515.4 17.0 %convolution_convert_fusion.5 = bf16[16,256,256]{2,1,0:T(8,128)(2,1)} fusion(bf16[16,256,1664]{2,1,0:T(8,128)(2,1)} %bitcast.128, bf16[16,256,1664]{2,1,0:T(8,128)(2,1)} %bitcast.131), kind=kOutput, calls=%fused_computation.73 | convolution fusion | flops 3490709504 | bytes 29360128 | tf_op jit(solution)/shard_map/qic,qjc->qij/dot_general | solution.py:380
  533.5 3.8 add_convert_fusion.10
  538.2 1.4 copy-done.4
  539.9 1.0 add_convert_fusion.9
  540.9 2.8 fusion.377
  544.2 0.9 add_convert_fusion.8
  545.2 2.7 fusion.378
  548.6 1.3 copy-done.3
  549.9 2.7 fusion.379
  552.6 13.5 %convolution_convert_fusion.1 = bf16[16,256,1664]{2,1,0:T(8,128)(2,1)} fusion(bf16[16,256,1664]{2,1,0:T(8,128)(2,1)} %bitcast.129, bf16[16,256,256]{2,1,0:T(8,128)(2,1)S(1)} %add_convert_fusion.10, bf16[16,256,256]{2,1,0:T(8,128)(2,1)} %copy-done.3), kind=kOutput, calls=%fused_computation.2 | convolution fusion | flops 4034396160 | bytes 31457280 | tf_op jit(solution)/shard_map/qji,qjc->qic/dot_general | solution.py:380
  568.8 2.0 convolution_select_fusion.3
  571.6 3.0 fusion.55
  574.6 3.0 fusion.61
  577.6 3.0 fusion.67
  580.6 3.0 fusion.73
  583.6 3.0 fusion.79
  586.6 3.2 fusion.85
  589.8 2.7 copy.29
  592.5 1.6 copy.30
  594.1 10.3 %copy.22 = bf16[8,16,32,1664]{3,2,1,0:T(8,128)(2,1)} copy(bf16[8,16,32,1664]{3,2,0,1:T(8,128)(2,1)} %bitcast.124) | data formatting | bytes 27262976 | tf_op jit(solution)/shard_map/transpose | solution.py:441
  604.4 20.9 %convolution_convert_fusion.2 = bf16[8,512,512]{2,1,0:T(8,128)(2,1)} fusion(bf16[8,512,1664]{2,1,0:T(8,128)(2,1)} %bitcast.125, f32[8,512,1664]{2,1,0:T(8,128)} %copy.24, bf16[8,512,1664]{2,1,0:T(8,128)(2,1)} %get-tuple-element.11), kind=kOutput, calls=%fused_computation.62 | convolution fusion | flops 7001866240 | bytes 58720256 | tf_op jit(solution)/shard_map/nic,njc->nij/dot_general | solution.py:380
  625.3 2.8 pad_maximum_fusion.part_ref
  628.1 40.1 %shard_map.47 = f32[512,704]{1,0:T(8,128)S(1)} custom-call(bf16[8,512,704]{2,1,0:T(8,128)(2,1)S(1)} %pad_maximum_fusion.part_ref), custom_call_target="tpu_custom_call" | custom-call | tf_op jit(solution)/shard_map/pallas_call | solution.py:320
  668.2 3.0 convolution_convert_fusion.9
  671.2 1.5 convolution_convert_fusion.8
  676.2 1.0 fusion.133
  677.2 1.0 fusion.135
  679.2 1.0 fusion.129
  680.3 1.8 fusion.131
  682.1 1.9 fusion.51
  684.0 2.4 fusion.125
  686.4 1.7 fusion.127
  689.3 0.9 copy-done.25
  690.3 37.6 %all-reduce.3.cloned.1.call-done = f32[7,512,64]{1,2,0:T(8,128)} async-done(((f32[7,512,64]{1,2,0:T(8,128)}), f32[7,512,64]{1,2,0:T(8,128)}) %all-reduce.3.cloned.1.call-update) | async-done | bytes 917520 | tf_op jit(solution)/shard_map/psum | solution.py:456
  727.8 2.2 copy.59
  (124 shorter events, 14.5 us)
Async XLA Ops:
  6.5 10.2 %copy-start.41 = (f32[4,104]{1,0:T(4,128)S(1)}, f32[4,104]{1,0:T(4,128)}, u32[]{:S(2)}) copy-start(f32[4,104]{1,0:T(4,128)} %param.5) | copy-start | bytes 4996
  6.5 721.3 %all-reduce.3.cloned.1.call-start = ((), (), s32[]{:S(2)}) async-start(), calls=%async_computation | async-start | bytes 1835008 | tf_op jit(solution)/shard_map/psum | solution.py:456
  6.5 672.7 %copy-start.34 = (s32[512]{0:T(512)}, s32[512]{0:T(512)S(1)}, u32[]{:S(2)}) copy-start(s32[512]{0:T(512)S(1)} %get-tuple-element.44) | copy-start | bytes 6148
  6.6 672.7 %copy-start.36 = (s32[512]{0:T(512)}, s32[512]{0:T(512)S(1)}, u32[]{:S(2)}) copy-start(s32[512]{0:T(512)S(1)} %get-tuple-element.47) | copy-start | bytes 6148
  6.6 672.6 %copy-start.32 = (pred[512]{0:T(512)(128)(4,1)}, pred[512]{0:T(512)(128)(4,1)S(1)}, u32[]{:S(2)}) copy-start(pred[512]{0:T(512)(128)(4,1)S(1)} %get-tuple-element.49) | copy-start | bytes 1540
  6.6 672.6 %copy-start.39 = (pred[512]{0:T(512)(128)(4,1)}, pred[512]{0:T(512)(128)(4,1)S(1)}, u32[]{:S(2)}) copy-start(pred[512]{0:T(512)(128)(4,1)S(1)} %get-tuple-element.48) | copy-start | bytes 1540
  346.1 4.4 slice-start
  352.0 5.4 copy-start.6
  352.0 5.3 copy-start.8
  352.0 5.3 copy-start.9
  357.3 4.6 copy-start.10
  361.9 4.6 copy-start.12
  366.6 4.5 copy-start.11
  371.0 4.6 copy-start.38
  532.8 0.7 copy-start.15
  532.8 5.4 copy-start.17
  532.8 5.4 copy-start.19
  532.8 10.8 %copy-start.21 = (f32[256,256]{1,0:T(8,128)}, f32[256,256]{1,0:T(8,128)S(1)}, u32[]{:S(2)}) copy-start(f32[256,256]{1,0:T(8,128)S(1)} %get-tuple-element.32) | copy-start | bytes 786436
  532.9 10.8 %copy-start.23 = (f32[256,256]{1,0:T(8,128)}, f32[256,256]{1,0:T(8,128)S(1)}, u32[]{:S(2)}) copy-start(f32[256,256]{1,0:T(8,128)S(1)} %get-tuple-element.34) | copy-start | bytes 786436
  532.9 4.5 copy-start.13
  537.4 2.2 copy-start.4
  537.4 2.5 copy-start.7
  540.9 3.3 copy-start.5
  548.6 1.3 copy-start.3
  552.6 13.5 %copy-start.31 = (bf16[512,64]{0,1:T(8,128)(2,1)S(1)}, bf16[512,64]{0,1:T(8,128)(2,1)}, u32[]{:S(2)}) copy-start(bf16[512,64]{0,1:T(8,128)(2,1)} %get-tuple-element.23) | copy-start | bytes 196612
  566.6 0.8 copy-start.30
  568.0 0.8 copy-start.29
  568.8 102.4 %copy-start.26 = (bf16[512,512]{1,0:T(8,128)(2,1)}, bf16[512,512]{1,0:T(8,128)(2,1)S(1)}, u32[]{:S(2)}) copy-start(bf16[512,512]{1,0:T(8,128)(2,1)S(1)} %fusion.48) | copy-start | bytes 1572868
  568.8 2.7 copy-start.2
  568.8 2.8 copy-start.24
  571.6 3.0 copy-start.22
  571.6 6.0 copy-start.1
  571.6 6.0 copy-start.20
  574.6 6.1 copy-start.18
  577.6 6.0 copy-start
  577.6 6.0 copy-start.16
  604.4 20.9 %copy-start.14 = (bf16[8,16,32,192]{3,2,1,0:T(8,128)(2,1)S(1)}, bf16[8,16,32,192]{3,2,1,0:T(8,128)(2,1)}, u32[]{:S(2)}) copy-start(bf16[8,16,32,192]{3,2,1,0:T(8,128)(2,1)} %copy.30) | copy-start | bytes 4718596
  674.0 0.9 copy-start.28
  677.2 1.5 copy-start.27
  680.3 3.7 copy-start.33
  680.3 3.7 copy-start.35
  684.0 2.4 copy-start.37
  684.0 2.4 copy-start.40
  689.3 0.9 copy-start.25
Sparse Core Ops, SparseCore 0:
  690.4 37.3 all-reduce.2

commit v2 on v1

--- a/solution.py
+++ b/solution.py
@@ -170,8 +170,8 @@
 
 
 def exchange_kernel(
-    n, codes_ref, up_ref, mix_ref, scale_ref,
-    codes_out, up_out, mix_out, scale_out,
+    n, codes_ref, up_ref, mix_ref, inner_ref, scale_ref,
+    codes_out, up_out, mix_out, inner_out, scale_out,
     send_sem, recv_sem, own_sem,
 ):
     index = lax.axis_index("fsdp")
@@ -198,6 +198,7 @@
     local = [
         pltpu.make_async_copy(mix_ref, mix_out.at[me], own_sem.at[0]),
         pltpu.make_async_copy(scale_ref, scale_out.at[me], own_sem.at[1]),
+        pltpu.make_async_copy(inner_ref, inner_out.at[me], own_sem.at[4]),
         pltpu.make_async_copy(codes_ref.at[:, columns(me)], codes_out.at[me], own_sem.at[2]),
         pltpu.make_async_copy(up_ref.at[:, :, columns(me)], up_out.at[:, me], own_sem.at[3]),
     ]
@@ -205,7 +206,10 @@
         copy.start()
     copies, mixes = [], {}
     for mask in list(range(2, n, 2)) + [1]:
-        mixes[mask] = send(0, mask, mix_ref, mix_out.at[me], mask)
+        mixes[mask] = [
+            send(0, mask, mix_ref, mix_out.at[me], mask),
+            send(4, mask, inner_ref, inner_out.at[me], mask),
+        ]
     order = sorted(range(1, n), key=lambda mask: -mask)
     for mask in order:
         copies.append(send(1, mask, scale_ref, scale_out.at[me], mask))
@@ -216,15 +220,16 @@
         src = codes_ref.at[:, columns(flipped(me, mask))]
         copies.append(send(3, mask, src, codes_out.at[me], mask))
     for mask in range(2, n, 2):
-        mixes[mask].wait()
-        block = mix_out.at[flipped(me, mask)]
-        copies.append(send(0, mask + 1, block, block, 1))
-    mixes[1].wait()
+        for kind, out in ((0, mix_out), (4, inner_out)):
+            mixes[mask][kind // 4].wait()
+            block = out.at[flipped(me, mask)]
+            copies.append(send(kind, mask + 1, block, block, 1))
+    copies += mixes[1]
     for copy in copies + local:
         copy.wait()
 
 
-def exchange(n, codes, upstream, mixing, scales, half):
+def exchange(n, codes, upstream, mixing, inner, scales, half):
     rows, cols = codes.shape
     wide = cols // n
     parts = rows // half
@@ -233,33 +238,35 @@
         jax.ShapeDtypeStruct((n, rows, wide), codes.dtype),
         jax.ShapeDtypeStruct((parts, n, half, wide), upstream.dtype),
         jax.ShapeDtypeStruct((n,) + mixing.shape, mixing.dtype),
+        jax.ShapeDtypeStruct((n,) + inner.shape, inner.dtype),
         jax.ShapeDtypeStruct((n,) + scales.shape, scales.dtype),
     )
     return pl.pallas_call(
         functools.partial(exchange_kernel, n),
         out_shape=shapes,
-        in_specs=[any_space] * 4,
-        out_specs=[any_space] * 4,
+        in_specs=[any_space] * 5,
+        out_specs=[any_space] * 5,
         scratch_shapes=[
-            pltpu.SemaphoreType.DMA((4, n)),
-            pltpu.SemaphoreType.DMA((4, n)),
-            pltpu.SemaphoreType.DMA((4,)),
+            pltpu.SemaphoreType.DMA((5, n)),
+            pltpu.SemaphoreType.DMA((5, n)),
+            pltpu.SemaphoreType.DMA((5,)),
         ],
         compiler_params=pltpu.CompilerParams(collective_id=0, has_side_effects=True),
         cost_estimate=pl.CostEstimate(
             flops=0, bytes_accessed=8 * rows * cols, transcendentals=0
         ),
-    )(codes, upstream.reshape(parts, half, cols), mixing, scales)
-
-
-def reduce_kernel(n, part_ref, out_ref, near, held, far, send_sem, recv_sem):
+    )(codes, upstream.reshape(parts, half, cols), mixing, inner, scales)
+
+
+def reduce_kernel(n, pair, part_ref, out_ref, near, held, far, mine, cross, send_sem, recv_sem):
     index = lax.axis_index("fsdp")
     me = lax.rem(index, n)
     device = lambda mask: {"fsdp": index - me + flipped(me, mask)}
     masks = list(range(0, n, 2))
-    greet([device(mask) for mask in [1] + masks[1:]])
+    across = {"col": 1 - lax.axis_index("col")} if pair else None
+    greet([device(mask) for mask in [1] + masks[1:]] + ([across] if pair else []))
     rows = out_ref.shape[0]
-    step = 64
+    step = 32
 
     def send(slot, src, dst, to):
         copy = pltpu.make_async_remote_copy(
@@ -267,7 +274,7 @@
             dst_ref=dst,
             send_sem=send_sem.at[slot],
             recv_sem=recv_sem.at[slot],
-            device_id=device(to),
+            device_id=to,
             device_id_type=MESH,
         )
         copy.start()
@@ -275,7 +282,7 @@
 
     order = masks[::-1]
     first = {
-        mask: send(mask, part_ref.at[flipped(me, mask + 1)], near.at[mask // 2], 1)
+        mask: send(mask, part_ref.at[flipped(me, mask + 1)], near.at[mask // 2], device(1))
         for mask in order
     }
     second = []
@@ -297,7 +304,7 @@
         lax.fori_loop(0, rows // step, add, 0)
         if mask:
             second.append(
-                send(mask + 1, held.at[mask // 2 - 1], far.at[mask // 2 - 1], mask)
+                send(mask + 1, held.at[mask // 2 - 1], far.at[mask // 2 - 1], device(mask))
             )
     for copy in second:
         copy.wait_recv()
@@ -307,18 +314,40 @@
         total = out_ref[at]
         for slot in range(n // 2 - 1):
             total = total + far[slot, at].astype(jnp.float32)
-        out_ref[at] = total
+        if pair:
+            mine[at] = total.astype(mine.dtype)
+        else:
+            out_ref[at] = total
         return carry
 
-    lax.fori_loop(0, rows // step, finish, 0)
+    if not pair:
+        lax.fori_loop(0, rows // step, finish, 0)
+    else:
+        pieces = 4
+        span = rows // pieces
+        third = []
+        for piece in range(pieces):
+            lax.fori_loop(piece * span // step, (piece + 1) * span // step, finish, 0)
+            at = pl.ds(piece * span, span)
+            third.append(send(n + piece, mine.at[at], cross.at[at], across))
+        for copy in third:
+            copy.wait_recv()
+
+        def join(i, carry):
+            at = pl.ds(pl.multiple_of(i * step, step), step)
+            out_ref[at] = mine[at].astype(jnp.float32) + cross[at].astype(jnp.float32)
+            return carry
+
+        lax.fori_loop(0, rows // step, join, 0)
+        second += third
     for copy in list(first.values()) + second:
         copy.wait_send()
 
 
-def reduce_parts(n, parts):
+def reduce_parts(n, pair, parts):
     _, rows, wide = parts.shape
     return pl.pallas_call(
-        functools.partial(reduce_kernel, n),
+        functools.partial(reduce_kernel, n, pair),
         out_shape=jax.ShapeDtypeStruct((rows, wide), jnp.float32),
         in_specs=[pl.BlockSpec(memory_space=pltpu.VMEM)],
         out_specs=pl.BlockSpec(memory_space=pltpu.VMEM),
@@ -326,13 +355,58 @@
             pltpu.VMEM((n // 2, rows, wide), parts.dtype),
             pltpu.VMEM((n // 2 - 1, rows, wide), parts.dtype),
             pltpu.VMEM((n // 2 - 1, rows, wide), parts.dtype),
-            pltpu.SemaphoreType.DMA((n,)),
-            pltpu.SemaphoreType.DMA((n,)),
+            pltpu.VMEM((rows, wide), parts.dtype),
+            pltpu.VMEM((rows, wide), parts.dtype),
+            pltpu.SemaphoreType.DMA((n + 4,)),
+            pltpu.SemaphoreType.DMA((n + 4,)),
         ],
         compiler_params=pltpu.CompilerParams(
             collective_id=1, has_side_effects=True, vmem_limit_bytes=40 * 2**20
         ),
     )(parts)
+
+
+def inner_kernel(codes_ref, scale_ref, mat_ref, grad_ref, val_ref, gram_ref, base):
+    rows, wide = base.shape
+    half = val_ref.shape[2]
+    side = rows // scale_ref.shape[1]
+    for block in range(rows // side):
+        at = slice(block * side, (block + 1) * side)
+        scaled = codes_ref[0, at].astype(jnp.float32) * scale_ref[0, block : block + 1]
+        base[at] = scaled.astype(base.dtype)
+    count = LANES // half
+    for block in range(rows // LANES):
+        at = slice(block * LANES, (block + 1) * LANES)
+        places = slice(block * count, (block + 1) * count)
+        out = jnp.dot(mat_ref[0, at], base[...], preferred_element_type=jnp.float32)
+        val_ref[places, 0] = out.astype(val_ref.dtype).reshape(count, half, wide)
+        grad = grad_ref[places, 0].reshape(LANES, wide)
+        gram = lax.dot_general(
+            grad, base[...], (((1,), (1,)), ((), ())), preferred_element_type=jnp.float32
+        )
+        gram_ref[0, at] = gram.astype(gram_ref.dtype)
+
+
+def inner_pass(codes, scale, mats, grad):
+    n, rows, wide = codes.shape
+    parts, _, half, _ = grad.shape
+    own = lambda shape: pl.BlockSpec((1,) + shape, lambda i: (i, 0, 0))
+    spread_out = pl.BlockSpec((parts, 1, half, wide), lambda i: (0, i, 0, 0))
+    return pl.pallas_call(
+        inner_kernel,
+        grid=(n,),
+        out_shape=(
+            jax.ShapeDtypeStruct(grad.shape, jnp.bfloat16),
+            jax.ShapeDtypeStruct((n, rows, rows), jnp.bfloat16),
+        ),
+        in_specs=[own((rows, wide)), own(scale.shape[1:]), own((rows, rows)), spread_out],
+        out_specs=(spread_out, own((rows, rows))),
+        scratch_shapes=[pltpu.VMEM((rows, wide), jnp.bfloat16)],
+        compiler_params=pltpu.CompilerParams(vmem_limit_bytes=48 * 2**20),
+        cost_estimate=pl.CostEstimate(
+            flops=4 * n * rows * rows * wide, bytes_accessed=6 * n * rows * wide, transcendentals=0
+        ),
+    )(codes, scale, mats, grad)
 
 
 def block_mask(count, half, bit, side, dtype):
@@ -361,14 +435,15 @@
     return (wide[0] + wide[1]).astype(jnp.bfloat16)
 
 
-def gather_back(full, bit, half):
+def gather_back(full, bit, half, kind, precision):
     count = full.shape[-1]
-    eye = repeat_eye(count, half, jnp.float32)
+    eye = repeat_eye(count, half, kind)
+    full = full.astype(kind)
     return jnp.concatenate(
         [
             jnp.einsum(
-                "...tc,sc->...ts", full * block_mask(count, half, bit, side, jnp.float32), eye,
-                preferred_element_type=jnp.float32, precision=lax.Precision.HIGHEST,
+                "...tc,sc->...ts", full * block_mask(count, half, bit, side, kind), eye,
+                preferred_element_type=jnp.float32, precision=precision,
             )
             for side in range(2)
         ],
@@ -390,7 +465,7 @@
     return prefix
 
 
-def level_grads(gram, mats, prefix, half):
+def level_grads(gram, mats, prefix, half, kind, precision):
     out = [None] * len(mats)
     left = gram
     for bit in reversed(range(len(mats))):
@@ -398,7 +473,7 @@
         if bit:
             full = product("...ij,...kj->...ik", left, prefix[bit])
             left = product("...ji,...jk->...ik", mats[bit], left)
-        out[bit] = gather_back(full, bit, half)
+        out[bit] = gather_back(full, bit, half, kind, precision)
     return out
 
 
@@ -420,40 +495,39 @@
             for level in range(levels)
         ]
     )
-    packed = mixing.reshape(levels * rows * block // LANES, LANES)
+    own = [spread(mixing[level], level) for level in range(low)]
+    own_prefix = chain(own)
+    packed = mixing[low:].reshape((levels - low) * rows * block // LANES, LANES)
     padded = jnp.pad(scales, ((0, -scale_rows % 8), (0, -scale_cols % LANES)))
-    codes_all, up, packed_all, scales_all = exchange(n, codes, upstream, packed, padded, half)
-    mix_all = packed_all.reshape(n, levels, rows, block)
-
+    codes_all, up, packed_all, inner_all, scales_all = exchange(
+        n, codes, upstream, packed, own_prefix[-1], padded, half
+    )
     scale = lax.dynamic_slice_in_dim(scales_all[:, :scale_rows], me * (wide // side), wide // side, 2)
-    base = codes_all.astype(jnp.float32).reshape(n, scale_rows, side, wide // side, side)
-    base = (base * scale[:, :, None, :, None]).astype(jnp.bfloat16).reshape(n, rows, wide)
-
-    inner = [spread(mix_all[:, level], level) for level in range(low)]
-    inner_prefix = chain(inner)
-    outer_mix = mix_all[:, low:].reshape(n, levels - low, parts, half, block)
+    scale = jnp.repeat(scale, side, axis=2)
+
+    outer_mix = packed_all.reshape(n, levels - low, parts, half, block)
     outer_mix = outer_mix.transpose(1, 2, 0, 3, 4).reshape(levels - low, parts, n * half, block)
     outer = [spread(outer_mix[bit], bit) for bit in range(levels - low)]
     outer_prefix = chain(outer)
 
     up = up.reshape(parts, n * half, wide)
     grad = product("qji,qjc->qic", outer_prefix[-1], up).astype(jnp.bfloat16)
-    grad = grad.reshape(parts, n, half, wide).transpose(1, 0, 2, 3).reshape(n, rows, wide)
-    values = product("nij,njc->nic", inner_prefix[-1], base).astype(jnp.bfloat16)
-    values = values.reshape(n, parts, half, wide).transpose(1, 0, 2, 3)
-    values = values.reshape(parts, n * half, wide)
-    inner_gram = product("nic,njc->nij", grad, base)
-    outer_gram = product("qic,qjc->qij", up, values)
-    upper = jnp.concatenate(level_grads(outer_gram, outer, outer_prefix, half), axis=-1)
+    values, inner_gram = inner_pass(
+        codes_all, scale, inner_all, grad.reshape(parts, n, half, wide)
+    )
+    outer_gram = product("qic,qjc->qij", up, values.reshape(parts, n * half, wide))
+    upper = level_grads(outer_gram, outer, outer_prefix, half, jnp.bfloat16, None)
+    upper = jnp.concatenate(upper, axis=-1).astype(jnp.bfloat16)
     upper = upper.reshape(parts, n, half, -1).transpose(1, 0, 2, 3).reshape(n, rows, -1)
 
-    partial = jnp.concatenate([inner_gram, upper], axis=2).astype(jnp.bfloat16)
-    total = reduce_parts(n, partial)
-    own = [spread(mixing[level], level) for level in range(low)]
-    lower = level_grads(total[:, :rows], own, chain(own), half)
+    pair = lax.axis_size("col") == 2
+    total = reduce_parts(n, pair, jnp.concatenate([inner_gram, upper], axis=2))
+    lower = level_grads(
+        total[:, :rows], own, own_prefix, half, jnp.float32, lax.Precision.HIGHEST
+    )
     upper = total[:, rows:].reshape(rows, levels - low, block).transpose(1, 0, 2)
     stacked = jnp.concatenate([jnp.stack(lower), upper], axis=0)
-    return lax.psum(stacked, "col")
+    return stacked if pair else lax.psum(stacked, "col")
 
 
 def body(codes, scales, factors, upstream):

time: 748 us -> 540 us (0.72)
  matrix products: 191 us -> 64.2 us
  local copies, waits for them, and re-layouts: 119 us -> 37.3 us
  Pallas kernels: 359 us -> 422 us
  waiting for transfers between devices: 37.6 us -> 0 us
  between operations: 14.3 us -> 1.38 us
  other arithmetic: 16.9 us -> 6.1 us
    dot_general x19 -> x16, matrix products: 125 us -> 41.3 us  [product(): jnp.einsum(spec, left.astype(jnp.bfloat16), right.astype(jnp.bfloat16), p...]
    mul x3 -> x0, local copies, waits for them, and re-layouts: 67.2 us -> none  [per_device_columns(): base * scale[:, :, None, :, None]]
    pallas_call x1 -> x2, Pallas kernels: 40.1 us -> 91.5 us  [the longest x1 59.8 us: reduce_parts(): pl.pallas_call(functools.partial(reduce_kernel, n, pair), out_shape=jax.S...]
    psum x1 -> x0, waiting for transfers between devices: 37.6 us -> none  [per_device_columns(): return lax.psum(stacked, 'col')]
    dot_general x17 -> x14, matrix products: 37.2 us -> 10.7 us  [spread(): jnp.einsum('...ts,sc->...tc', mix[..., side * half:(side + 1) * half], ey...]
    transpose x3 -> x0, local copies, waits for them, and re-layouts: 22.1 us -> none  [the longest x1 10.3 us: per_device_columns(): grad.reshape(parts, n, half, wide).transpose(1, 0, 2, 3)]
    dot_general x14, matrix products: 28.9 us -> 12.2 us  [gather_back(): jnp.einsum('...tc,sc->...ts', full * block_mask(count, half, bit, side, k...]
    concatenate x1 -> x13, local copies, waits for them, and re-layouts: 2.73 us -> 17.3 us  [per_device_columns(): upper = jnp.concatenate(upper, axis=-1).astype(jnp.bfloat16)]
  transfers between devices with their start and end apart: 1 -> 0, of which waited for: 1 -> 0; matrix products, arithmetic and copies ran while one was open for 0% -> 0% of each run, Pallas kernels for 0% -> 0%
where the time goes in v2:
time: 540 us; the launch traced here: 531 us
  Pallas kernels  422 us (78%)
  matrix products  64.2 us (12%)
  local copies, waits for them, and re-layouts  37.3 us (7%)
  other arithmetic  6.1 us (1%)
    pallas_call x1, Pallas kernels, exchange(): pl.pallas_call(functools.partial(exchange_kernel, n), out_shape=shapes, i...  330 us
    pallas_call x1, Pallas kernels, reduce_parts(): pl.pallas_call(functools.partial(reduce_kernel, n, pair), out_shape=jax.S...  59.8 us
    dot_general x16, matrix products, product(): jnp.einsum(spec, left.astype(jnp.bfloat16), right.astype(jnp.bfloat16), p...  41.3 us
    pallas_call x1, Pallas kernels, inner_pass(): pl.pallas_call(inner_kernel, grid=(n,), out_shape=(jax.ShapeDtypeStruct(g...  31.7 us
    concatenate x13, local copies, waits for them, and re-layouts, per_device_columns(): upper = jnp.concatenate(upper, axis=-1).astype(jnp.bfloat16)  17.3 us
    dot_general x14, matrix products, gather_back(): jnp.einsum('...tc,sc->...ts', full * block_mask(count, half, bit, side, k...  12.2 us

profile of v2, /device:TPU:0, one launch (start us, length us, event | category | flops | bytes accessed | tf_op | source)
XLA Modules:
  0.0 530.7 jit_solution(18281915962285538000)
XLA Ops:
  0.1 1.3 pad.4.scale_ref
  1.6 1.1 add_convert_fusion.5
  2.9 0.9 reshape.1331.mix_ref
  4.7 0.5 convolution_select_fusion.3
  5.2 0.8 fusion.21
  6.0 0.5 convolution_select_fusion.5
  6.5 0.8 fusion.20
  7.3 0.5 convolution_select_fusion.7
  7.8 0.8 fusion.19
  9.1 0.8 copy-done.9
  10.4 0.8 copy-done.7
  11.2 1.2 convolution_convert_fusion.9.inner_ref
  12.4 1.9 fusion.116
  14.4 330.2 %shard_map.46 = (bf16[8,512,1664]{2,1,0:T(8,128)(2,1)}, bf16[16,8,32,1664]{3,2,1,0:T(8,128)(2,1)}, bf16[8,768,128]{2,1,0:T(8,128)(2,1)}, bf16[8,512,512]{2,1,0:T(8,128)(2,1)}, f32[8,8,128]{2,1,0:T(8,128)}) custom-call(bf16[512,13312]{1,0:T(8,128)(2,1)} %codes_ref.1, bf16[16,32,13312]{2,1,0:T(8,128)(2,1)} %bitcast.110, bf16[768,128]{1,0:T(8,128)(2,1)} %reshape.1331.mix_ref, ...), custom_call_target="tpu_custom_call" | custom-call | bytes 54525952 | tf_op jit(solution)/shard_map/pallas_call | solution.py:244
  344.6 0.8 slice.100
  345.7 3.9 reshape.1333
  349.6 0.9 copy.46
  350.5 0.5 fusion.286
  351.1 0.7 fusion.57
  352.1 0.9 add_convert_fusion.1
  353.1 0.7 fusion.54
  354.4 0.9 add_convert_fusion
  355.4 0.7 convolution_convert_fusion.5
  356.1 0.6 copy-done.4
  356.8 0.7 fusion.60
  357.8 2.2 add_convert_fusion.2
  360.0 14.0 %convolution_convert_fusion = bf16[16,256,1664]{2,1,0:T(8,128)(2,1)} fusion(bf16[16,256,1664]{2,1,0:T(8,128)(2,1)} %bitcast.107, bf16[16,256,256]{2,1,0:T(8,128)(2,1)} %add_convert_fusion.2, bf16[16,256,256]{2,1,0:T(8,128)(2,1)S(1)} %convolution_convert_fusion.5), kind=kOutput, calls=%fused_computation | convolution fusion | flops 4034396160 | bytes 31457280 | tf_op jit(solution)/shard_map/qji,qjc->qic/dot_general | solution.py:455
  374.1 31.7 %shard_map.47 = (bf16[16,8,32,1664]{3,2,1,0:T(8,128)(2,1)}, bf16[8,512,512]{2,1,0:T(8,128)(2,1)S(1)}) custom-call(bf16[8,512,1664]{2,1,0:T(8,128)(2,1)} %get-tuple-element.12.codes_ref, f32[8,4,1664]{2,1,0:T(4,128)S(1)} %copy.27.scale_ref, bf16[8,512,512]{2,1,0:T(8,128)(2,1)} %get-tuple-element.14.mat_ref, bf16[16,8,32,1664]{3,2,1,0:T(8,128)(2,1)} %bitcast.109), custom_call_target="tpu_custom_call" | custom-call | flops 13958643712 | bytes 40894464 | tf_op jit(solution)/shard_map/pallas_call | solution.py:395
  405.8 2.0 copy-done
  407.8 16.9 %convolution_convert_fusion.6 = bf16[16,256,256]{2,1,0:T(8,128)(2,1)} fusion(bf16[16,256,1664]{2,1,0:T(8,128)(2,1)} %bitcast.108, bf16[16,256,1664]{2,1,0:T(8,128)(2,1)} %bitcast.120), kind=kOutput, calls=%fused_computation.45 | convolution fusion | flops 3490709504 | bytes 29360128 | tf_op jit(solution)/shard_map/qic,qjc->qij/dot_general | solution.py:455
  424.7 2.5 convolution_convert_fusion.1
  427.5 0.8 convolution_convert_fusion.4
  428.3 0.8 copy-done.5
  429.1 0.7 convolution_convert_fusion.2
  429.9 0.8 copy-done.3
  430.7 0.8 convolution_convert_fusion.3
  431.6 0.7 fusion.26
  432.5 0.7 fusion.23
  433.3 0.7 fusion.32
  434.0 0.7 fusion.29
  434.7 0.7 fusion.38
  435.4 0.7 fusion.35
  436.6 0.9 copy.34
  437.9 1.6 copy.35
  439.9 1.5 copy.32
  441.9 1.6 copy.33
  444.0 1.6 copy.30
  446.0 1.6 copy.31
  447.6 6.0 %concatenate.41 = bf16[16,8,32,192]{3,2,0,1:T(8,128)(2,1)S(1)} concatenate(bf16[16,8,32,32]{3,2,0,1:T(8,128)(2,1)} %copy.30, bf16[16,8,32,32]{3,2,0,1:T(8,128)(2,1)} %copy.31, bf16[16,8,32,32]{3,2,0,1:T(8,128)(2,1)} %copy.32, bf16[16,8,32,32]{3,2,0,1:T(8,128)(2,1)} %copy.33, bf16[16,8,32,32]{3,2,0,1:T(8,128)(2,1)S(1)} %copy.34, bf16[16,8,32,32]{3,2,0,1:T(8,128)(2,1)} %copy.35), dimensions={3} | concatenate | bytes 3145728 | tf_op jit(solution)/shard_map/concatenate | solution.py:520
  453.5 2.8 pad_maximum_fusion.part_ref
  456.4 59.8 %shard_map.48 = f32[512,704]{1,0:T(8,128)S(1)} custom-call(bf16[8,512,704]{2,1,0:T(8,128)(2,1)S(1)} %pad_maximum_fusion.part_ref), custom_call_target="tpu_custom_call" | custom-call | tf_op jit(solution)/shard_map/pallas_call | solution.py:349
  516.6 0.6 copy-done.25
  518.2 1.0 fusion.66
  519.3 1.0 fusion.68
  520.8 0.6 copy-done.14
  521.8 0.9 fusion.74
  522.7 0.9 fusion.76
  523.6 1.0 fusion.70
  524.6 1.0 fusion.72
  525.7 0.5 fusion.105
  526.4 1.0 fusion.62
  527.4 1.0 fusion.64
  528.5 0.9 copy-done.31
  529.4 0.8 constant_dynamic-update-slice_fusion
  (115 shorter events, 9.8 us)
Async XLA Ops:
  0.0 3.8 copy-start.23
  0.0 7.8 %copy-start.38 = (pred[512]{0:T(512)(128)(4,1)}, pred[512]{0:T(512)(128)(4,1)S(1)}, u32[]{:S(2)}) copy-start(pred[512]{0:T(512)(128)(4,1)S(1)} %get-tuple-element.51) | copy-start | bytes 1540
  0.0 7.8 %copy-start.40 = (pred[512]{0:T(512)(128)(4,1)}, pred[512]{0:T(512)(128)(4,1)S(1)}, u32[]{:S(2)}) copy-start(pred[512]{0:T(512)(128)(4,1)S(1)} %get-tuple-element.52) | copy-start | bytes 1540
  1.5 6.3 %copy-start.32 = (s32[512]{0:T(512)}, s32[512]{0:T(512)S(1)}, u32[]{:S(2)}) copy-start(s32[512]{0:T(512)S(1)} %get-tuple-element.50) | copy-start | bytes 6148
  1.5 6.3 %copy-start.34 = (s32[512]{0:T(512)}, s32[512]{0:T(512)S(1)}, u32[]{:S(2)}) copy-start(s32[512]{0:T(512)S(1)} %get-tuple-element.47) | copy-start | bytes 6148
  1.6 6.3 %copy-start.36 = (s32[512]{0:T(512)}, s32[512]{0:T(512)S(1)}, u32[]{:S(2)}) copy-start(s32[512]{0:T(512)S(1)} %get-tuple-element.48) | copy-start | bytes 6148
  4.7 4.0 copy-start.11
  6.0 4.4 copy-start.15
  7.3 1.8 copy-start.24
  8.6 1.7 copy-start.13
  9.1 0.8 copy-start.9
  10.4 0.8 copy-start.7
  351.1 1.0 copy-start.21
  351.1 1.0 copy-start.22
  353.0 2.3 copy-start.2
  353.0 1.1 copy-start.19
  353.0 1.4 copy-start.20
  355.4 1.4 copy-start.4
  356.7 0.9 copy-start.17
  356.7 1.0 copy-start.18
  405.8 2.0 copy-start
  424.7 2.5 copy-start.1
  424.7 2.8 copy-start.6
  427.5 1.6 copy-start.5
  429.1 1.6 copy-start.3
  430.7 0.9 copy-start.30
  431.6 0.9 copy-start.29
  431.6 1.6 copy-start.28
  432.5 1.4 copy-start.27
  433.2 1.4 copy-start.26
  456.3 59.8 %copy-start.16 = (bf16[512,512]{1,0:T(8,128)(2,1)S(1)}, bf16[512,512]{1,0:T(8,128)(2,1)}, u32[]{:S(2)}) copy-start(bf16[512,512]{1,0:T(8,128)(2,1)} %copy-done.15) | copy-start | bytes 1572868
  516.1 1.0 copy-start.25
  516.2 1.5 copy-start.10
  517.2 1.0 copy-start.33
  517.2 1.0 copy-start.35
  517.2 1.0 copy-start.37
  517.2 1.0 copy-start.39
  517.2 1.0 copy-start.41
  519.2 1.0 copy-start.12
  520.3 1.0 copy-start.14
  524.6 1.0 copy-start.8
  528.5 0.9 copy-start.31

commit v3 on v2

--- a/solution.py
+++ b/solution.py
@@ -435,19 +435,22 @@
     return (wide[0] + wide[1]).astype(jnp.bfloat16)
 
 
-def gather_back(full, bit, half, kind, precision):
-    count = full.shape[-1]
-    eye = repeat_eye(count, half, kind)
-    full = full.astype(kind)
-    return jnp.concatenate(
+def gather_back(fulls, half, kind, precision):
+    count, picks = fulls[0].shape[-1], 2 * len(fulls)
+    masked = jnp.concatenate(
         [
-            jnp.einsum(
-                "...tc,sc->...ts", full * block_mask(count, half, bit, side, kind), eye,
-                preferred_element_type=jnp.float32, precision=precision,
-            )
+            full.astype(kind) * block_mask(count, half, bit, side, kind)
+            for bit, full in enumerate(fulls)
             for side in range(2)
         ],
         axis=-1,
+    )
+    shape = (picks * count, picks * half)
+    row = lax.broadcasted_iota(jnp.int32, shape, 0)
+    col = lax.broadcasted_iota(jnp.int32, shape, 1)
+    pick = ((row // count == col // half) & (row % half == col % half)).astype(kind)
+    return jnp.einsum(
+        "...tc,cs->...ts", masked, pick, preferred_element_type=jnp.float32, precision=precision
     )
 
 
@@ -473,8 +476,8 @@
         if bit:
             full = product("...ij,...kj->...ik", left, prefix[bit])
             left = product("...ji,...jk->...ik", mats[bit], left)
-        out[bit] = gather_back(full, bit, half, kind, precision)
-    return out
+        out[bit] = full
+    return gather_back(out, half, kind, precision)
 
 
 def per_device_columns(n, codes, scales, factors, upstream):
@@ -517,7 +520,7 @@
     )
     outer_gram = product("qic,qjc->qij", up, values.reshape(parts, n * half, wide))
     upper = level_grads(outer_gram, outer, outer_prefix, half, jnp.bfloat16, None)
-    upper = jnp.concatenate(upper, axis=-1).astype(jnp.bfloat16)
+    upper = upper.astype(jnp.bfloat16)
     upper = upper.reshape(parts, n, half, -1).transpose(1, 0, 2, 3).reshape(n, rows, -1)
 
     pair = lax.axis_size("col") == 2
@@ -525,8 +528,8 @@
     lower = level_grads(
         total[:, :rows], own, own_prefix, half, jnp.float32, lax.Precision.HIGHEST
     )
-    upper = total[:, rows:].reshape(rows, levels - low, block).transpose(1, 0, 2)
-    stacked = jnp.concatenate([jnp.stack(lower), upper], axis=0)
+    stacked = jnp.concatenate([lower, total[:, rows:]], axis=1)
+    stacked = stacked.reshape(rows, levels, block).transpose(1, 0, 2)
     return stacked if pair else lax.psum(stacked, "col")
 
 

time: 540 us -> 542 us (level); the launches traced: 531 us -> 541 us
  local copies, waits for them, and re-layouts: 37.3 us -> 14.8 us
  matrix products: 64.2 us -> 84.3 us
  other arithmetic: 6.1 us -> 20.2 us
    concatenate x14 -> x0, local copies, waits for them, and re-layouts: 18.1 us -> none  [the longest x13 17.3 us: per_device_columns(): upper = jnp.concatenate(upper, axis=-1).astype(jnp.bfloat16)]
    dot_general x16, matrix products: 41.3 us -> 55 us  [product(): jnp.einsum(spec, left.astype(jnp.bfloat16), right.astype(jnp.bfloat16), p...]
    unnamed x4 -> x5, other arithmetic: 0.05 us -> 8.69 us
    unnamed x84 -> x38, local copies, waits for them, and re-layouts: 10.1 us -> 2.28 us
    dot_general x14 -> x2, matrix products: 12.2 us -> 19.8 us  [gather_back(): jnp.einsum('...tc,cs->...ts', masked, pick, preferred_element_type=jnp.fl...]
where the time goes in v3:
time: 542 us; the launch traced here: 541 us
  Pallas kernels  421 us (78%)
  matrix products  84.3 us (16%)
  other arithmetic  20.2 us (4%)
  local copies, waits for them, and re-layouts  14.8 us (3%)
    pallas_call x1, Pallas kernels, exchange(): pl.pallas_call(functools.partial(exchange_kernel, n), out_shape=shapes, i...  330 us
    pallas_call x1, Pallas kernels, reduce_parts(): pl.pallas_call(functools.partial(reduce_kernel, n, pair), out_shape=jax.S...  59.5 us
    dot_general x16, matrix products, product(): jnp.einsum(spec, left.astype(jnp.bfloat16), right.astype(jnp.bfloat16), p...  55 us
    pallas_call x1, Pallas kernels, inner_pass(): pl.pallas_call(inner_kernel, grid=(n,), out_shape=(jax.ShapeDtypeStruct(g...  31.7 us
    dot_general x2, matrix products, gather_back(): jnp.einsum('...tc,cs->...ts', masked, pick, preferred_element_type=jnp.fl...  19.8 us

profile of v3, /device:TPU:0, one launch (start us, length us, event | category | flops | bytes accessed | tf_op | source)
XLA Modules:
  0.0 541.3 jit_solution(13512196176076383854)
XLA Ops:
  0.1 1.2 fusion.76
  1.3 0.5 convolution_select_fusion.7
  1.8 0.8 fusion.22
  2.6 0.4 convolution_select_fusion.1
  3.0 0.4 fusion.25
  3.4 0.4 convolution_convert_fusion.12
  3.9 0.5 convolution_select_fusion.5
  4.4 0.8 fusion.23
  5.2 0.4 convolution_convert_fusion.11
  5.7 0.5 convolution_select_fusion.3
  6.2 0.8 fusion.24
  7.0 1.2 convolution_convert_fusion.10.inner_ref
  8.3 1.1 add_convert_fusion.5
  9.4 0.2 copy.28
  9.7 0.9 reshape.1321.mix_ref
  10.6 0.6 pad.4.scale_ref
  11.1 330.1 %shard_map.46 = (bf16[8,512,1664]{2,1,0:T(8,128)(2,1)}, bf16[16,8,32,1664]{3,2,1,0:T(8,128)(2,1)}, bf16[8,768,128]{2,1,0:T(8,128)(2,1)}, bf16[8,512,512]{2,1,0:T(8,128)(2,1)}, f32[8,8,128]{2,1,0:T(8,128)}) custom-call(bf16[512,13312]{1,0:T(8,128)(2,1)} %codes_ref.1, bf16[16,32,13312]{2,1,0:T(8,128)(2,1)} %bitcast.82, bf16[768,128]{1,0:T(8,128)(2,1)} %reshape.1321.mix_ref, ...), custom_call_target="tpu_custom_call" | custom-call | bytes 54525952 | tf_op jit(solution)/shard_map/pallas_call | solution.py:244
  341.3 3.9 reshape.1323
  345.2 0.9 copy.72
  346.1 0.5 fusion.190
  346.7 0.7 fusion.42
  347.4 0.6 fusion.82
  348.0 0.9 add_convert_fusion
  348.9 0.7 fusion.45
  349.6 0.9 add_convert_fusion.1
  350.5 2.1 convolution_convert_fusion.5
  352.6 0.7 fusion.48
  353.3 0.9 add_convert_fusion.2
  354.3 13.7 %convolution_convert_fusion = bf16[16,256,1664]{2,1,0:T(8,128)(2,1)} fusion(bf16[16,256,1664]{2,1,0:T(8,128)(2,1)} %bitcast.79, bf16[16,256,256]{2,1,0:T(8,128)(2,1)S(1)} %add_convert_fusion.2, bf16[16,256,256]{2,1,0:T(8,128)(2,1)} %convolution_convert_fusion.5), kind=kOutput, calls=%fused_computation | convolution fusion | flops 4034396160 | bytes 31457280 | tf_op jit(solution)/shard_map/qji,qjc->qic/dot_general | solution.py:458
  368.1 0.1 broadcast_in_dim.2
  368.3 31.7 %shard_map.47 = (bf16[16,8,32,1664]{3,2,1,0:T(8,128)(2,1)}, bf16[8,512,512]{2,1,0:T(8,128)(2,1)S(1)}) custom-call(bf16[8,512,1664]{2,1,0:T(8,128)(2,1)} %get-tuple-element.12.codes_ref, f32[8,4,1664]{2,1,0:T(4,128)S(1)} %copy.37.scale_ref, bf16[8,512,512]{2,1,0:T(8,128)(2,1)} %get-tuple-element.14.mat_ref, bf16[16,8,32,1664]{3,2,1,0:T(8,128)(2,1)} %bitcast.81), custom_call_target="tpu_custom_call" | custom-call | flops 13958643712 | bytes 40894464 | tf_op jit(solution)/shard_map/pallas_call | solution.py:395
  400.0 2.0 copy-done
  402.0 16.7 %convolution_convert_fusion.6 = bf16[16,256,256]{2,1,0:T(8,128)(2,1)} fusion(bf16[16,256,1664]{2,1,0:T(8,128)(2,1)} %bitcast.80, bf16[16,256,1664]{2,1,0:T(8,128)(2,1)} %bitcast.92), kind=kOutput, calls=%fused_computation.55 | convolution fusion | flops 3490709504 | bytes 29360128 | tf_op jit(solution)/shard_map/qic,qjc->qij/dot_general | solution.py:458
  418.8 3.7 convolution_convert_fusion.4
  422.5 0.1 copy.40
  422.6 5.1 multiply_dynamic-update-slice_fusion.5
  427.7 0.1 copy.41
  427.8 3.5 multiply_dynamic-update-slice_fusion.4
  431.2 0.1 copy.42
  431.4 4.3 multiply_dynamic-update-slice_fusion.3
  435.7 0.1 copy.43
  435.8 3.6 multiply_dynamic-update-slice_fusion.2
  439.3 0.1 copy.44
  439.4 4.3 multiply_dynamic-update-slice_fusion.1
  443.9 3.4 multiply_dynamic-update-slice_fusion
  447.3 8.5 %convolution_convert_fusion.7 = bf16[16,256,192]{1,2,0:T(8,128)(2,1)} fusion(bf16[16,256,1536]{1,2,0:T(8,128)(2,1)} %multiply_dynamic-update-slice_fusion, s32[192]{0:T(256)S(1)} %get-tuple-element.78, s32[192]{0:T(256)S(1)} %get-tuple-element.81, s32[1536]{0:T(1024)S(1)} %get-tuple-element.71, s32[1536]{0:T(1024)S(1)} %get-tuple-element.73, ...), kind=kOutput, calls=%fused_computation.56 | convolution fusion | flops 2418769920 | bytes 14186880 | tf_op jit(solution)/shard_map/...tc,cs->...ts/dot_general | solution.py:452
  455.8 2.7 copy.47
  458.5 1.6 copy.48
  460.1 3.4 pad_maximum_fusion.part_ref
  463.6 59.5 %shard_map.48 = f32[512,704]{1,0:T(8,128)S(1)} custom-call(bf16[8,512,704]{2,1,0:T(8,128)(2,1)S(1)} %pad_maximum_fusion.part_ref), custom_call_target="tpu_custom_call" | custom-call | tf_op jit(solution)/shard_map/pallas_call | solution.py:349
  523.1 0.5 convolution_convert_fusion.9
  523.6 0.5 convolution_convert_fusion.8
  524.1 0.5 select_dynamic-update-slice_fusion.7
  524.6 0.3 select_dynamic-update-slice_fusion.6
  524.9 0.2 copy-done.12
  525.1 0.5 select_dynamic-update-slice_fusion.5
  525.6 0.7 select_dynamic-update-slice_fusion.4
  526.3 0.5 select_dynamic-update-slice_fusion.3
  526.9 0.7 select_dynamic-update-slice_fusion.2
  527.6 0.5 select_dynamic-update-slice_fusion.1
  528.1 0.7 select_dynamic-update-slice_fusion
  528.8 11.3 %fusion.1 = f32[512,256]{0,1:T(8,128)S(1)} fusion(f32[512,4096]{1,0:T(8,128)S(1)} %select_dynamic-update-slice_fusion, s32[256]{0:T(256)S(1)} %get-tuple-element.69, s32[256]{0:T(256)S(1)} %get-tuple-element.70, s32[4096]{0:T(1024)S(1)} %get-tuple-element.83, s32[4096]{0:T(1024)S(1)} %get-tuple-element.85, s32[256]{0:T(256)S(1)} %get-tuple-element.67, ...), kind=kOutput, calls=%fused_computation.28 | convolution fusion | flops 6449790976 | bytes 8991232 | tf_op jit(solution)/shard_map/...tc,cs->...ts/dot_general | solution.py:452
  540.1 0.2 copy.57
  540.3 1.0 pad_maximum_fusion.1
  (63 shorter events, 0.6 us)
Async XLA Ops:
  2.6 0.8 copy-start.13
  3.4 1.0 copy-start.11
  3.9 1.3 copy-start.7
  5.2 1.0 copy-start.15
  5.7 1.3 copy-start.5
  6.2 4.4 copy-start.18
  7.0 1.2 copy-start.9
  348.9 1.6 copy-start.2
  350.5 2.8 copy-start.4
  354.2 13.7 %copy-start.17 = (f32[8,8,128]{2,1,0:T(8,128)S(1)}, f32[8,8,128]{2,1,0:T(8,128)}, u32[]{:S(2)}) copy-start(f32[8,8,128]{2,1,0:T(8,128)} %get-tuple-element.13) | copy-start | bytes 98308
  400.0 2.0 copy-start
  427.7 3.7 copy-start.3
  435.7 3.8 copy-start.1
  463.6 59.5 %copy-start.10 = (bf16[512,512]{1,0:T(8,128)(2,1)S(1)}, bf16[512,512]{1,0:T(8,128)(2,1)}, u32[]{:S(2)}) copy-start(bf16[512,512]{1,0:T(8,128)(2,1)} %copy-done.9) | copy-start | bytes 1572868
  463.6 60.0 %copy-start.16 = (bf16[512,512]{1,0:T(8,128)(2,1)S(1)}, bf16[512,512]{1,0:T(8,128)(2,1)}, u32[]{:S(2)}) copy-start(bf16[512,512]{1,0:T(8,128)(2,1)} %copy-done.15) | copy-start | bytes 1572868
  463.6 60.5 %copy-start.14 = (bf16[512,512]{1,0:T(8,128)(2,1)S(1)}, bf16[512,512]{1,0:T(8,128)(2,1)}, u32[]{:S(2)}) copy-start(bf16[512,512]{1,0:T(8,128)(2,1)} %copy-done.13) | copy-start | bytes 1572868
  524.1 1.0 copy-start.12
  525.1 1.2 copy-start.8
  526.3 1.2 copy-start.6
